TPU v7x, 32 devices: a whole 2x2x4 slice. The times are simulated.
32 devices in a mesh: rows: 8 (over y, x, core), cp: 4 (over z).
Axes of the slice: x: 2, y: 2, z: 4, core: 2. Of those that a mesh axis runs over, the one named last changes fastest.
Arguments:
- tokens: bfloat16 [8, 2, 1024, 1024], P('rows', None, 'cp'), may hold values from -6 to 6
- doc_starts: int32 [8, 4], P('rows'), may hold values from 0 to 2047, as said below
- qkv_weight: bfloat16 [1024, 3072], P('rows', 'cp'), may hold values from -0.1875 to 0.1875
- out_weight: bfloat16 [1024, 1024], P('rows', 'cp'), may hold values from -0.1875 to 0.1875
- up_weight: bfloat16 [1024, 4096], P('rows', 'cp'), may hold values from -0.1875 to 0.1875
- down_weight: bfloat16 [4096, 1024], P('cp', 'rows'), may hold values from -0.09375 to 0.09375
- norm_gains: bfloat16 [4096], P(('rows', 'cp')), may hold values from 0.5 to 1.5
- cotangent: bfloat16 [8, 2, 1024, 1024], P('rows', None, 'cp'), may hold values from -6 to 6
Outputs:
- mixed: bfloat16 [8, 2, 1024, 1024], P('rows', None, 'cp')
- tokens_grad: float32 [8, 2, 1024, 1024], P('rows', None, 'cp')
- qkv_grad: float32 [1024, 3072], P('rows', 'cp')
- out_grad: float32 [1024, 1024], P('rows', 'cp')
- up_grad: float32 [1024, 4096], P('rows', 'cp')
- down_grad: float32 [4096, 1024], P('cp', 'rows')
- gains_grad: float32 [4096], P(('rows', 'cp'))
Inputs may be any that keep to these rules, and one draw needn't show every extreme that they name: `doc_starts`: in each row the 4 document starts rise strictly and the first is 0; a position belongs to the document with the last start at or before it.
All inputs are finite; a program needn't handle non-finite values.
Results may differ from a plain program's by a relative error of at most 0.023.
Values may be sent and summed in bfloat16 or wider, within the bound.
No kernel may reach another device: no remote copies, remote signals or barrier semaphores. Data moves between devices by JAX's collectives and lax.ppermute only.
A program may use at most 640 MiB of HBM per device.

v0:
```python
import functools
import math

import jax
import jax.numpy as jnp
from jax import lax
from jax.experimental import pallas as pl
from jax.experimental.layout import Layout, with_layout_constraint
from jax.experimental.pallas import tpu as pltpu
from jax.sharding import Mesh, PartitionSpec as P

HEADS = 16
HEAD_DIM = 64


NORM_EPS = 1e-05
MASKED = -1e30


def layer_norm(values):
    average = jnp.mean(values, axis=-1, keepdims=True)
    centred = values - average
    spread = jnp.mean(centred * centred, axis=-1, keepdims=True)
    return centred * lax.rsqrt(spread + NORM_EPS)


def norm_back(values, upstream):
    _, pull_back = jax.vjp(layer_norm, values)
    return pull_back(upstream)[0]


def gelu_tanh(values):
    return jax.nn.gelu(values, approximate=True)


def rotate(values, cosine, sine_part):
    half_width = values.shape[-1] // 2
    first_half = values[..., :half_width]
    second_half = values[..., half_width:]
    return jnp.concatenate(
        [
            first_half * cosine - second_half * sine_part,
            second_half * cosine + first_half * sine_part,
        ],
        axis=-1,
    )


def rounded(values):
    return lax.optimization_barrier(values.astype(jnp.bfloat16)).astype(jnp.float32)


def doc_start_of(starts, positions):
    return jnp.max(
        jnp.where(starts[:, None, :] <= positions[None, :, None], starts[:, None, :], 0), axis=-1
    )


def general_body(tokens, doc_starts, qkv_weight, out_weight, up_weight, down_weight, norm_gains, cotangent):
    rows_count = lax.axis_size("rows")
    cp_count = lax.axis_size("cp")
    qkv_rows, out_rows, up_rows, down_rows, gain_piece = (
        lax.all_gather(qkv_weight, "rows", axis=0, tiled=True),
        lax.all_gather(out_weight, "rows", axis=0, tiled=True),
        lax.all_gather(up_weight, "rows", axis=0, tiled=True),
        lax.all_gather(down_weight, "rows", axis=1, tiled=True),
        lax.all_gather(norm_gains, "rows", axis=0, tiled=True),
    )
    qkv_full, out_full, gain_mixed = (
        lax.all_gather(qkv_rows, "cp", axis=1, tiled=True),
        lax.all_gather(out_rows, "cp", axis=1, tiled=True),
        lax.all_gather(gain_piece, "cp", axis=0, tiled=True),
    )
    gain_full = jnp.transpose(gain_mixed.reshape(cp_count, rows_count, -1), (1, 0, 2)).reshape(-1)
    row_count, _, span_len, width = tokens.shape
    half_len = span_len * cp_count
    row_len = 2 * half_len
    queries_dev = 2 * span_len
    token_total = row_count * queries_dev
    group_total = row_count * row_len
    gain_rows = gain_full.astype(jnp.float32).reshape(4, width)
    score_scale = HEAD_DIM ** (-0.5)
    local_pos = lax.axis_index("cp") * span_len + jnp.arange(span_len, dtype=jnp.int32)
    query_pos = jnp.concatenate([local_pos, row_len - 1 - local_pos])
    half_pos = jnp.arange(half_len, dtype=jnp.int32)
    key_pos = jnp.concatenate([half_pos, row_len - 1 - half_pos])
    query_start = doc_start_of(doc_starts, query_pos)
    key_start = doc_start_of(doc_starts, key_pos)
    freq_index = jnp.arange(HEAD_DIM // 2, dtype=jnp.float32)
    inverse_freq = jnp.exp(-math.log(10000.0) * 2.0 * freq_index / HEAD_DIM)
    angles = (query_pos[None, :] - query_start).astype(jnp.float32)[..., None] * inverse_freq
    cosine = jnp.cos(angles)[:, :, None, :]
    sine_part = jnp.sin(angles)[:, :, None, :]
    head_shape = (row_count, queries_dev, HEADS, HEAD_DIM)
    flat_shape = (row_count, queries_dev, width)
    fold_shape = (row_count, 2, span_len, width)
    group_shape = (row_count, 2, half_len, width)
    full_shape = (row_count, row_len, HEADS, HEAD_DIM)
    inputs = tokens.astype(jnp.float32).reshape(flat_shape)
    normed_in = layer_norm(inputs)
    normed = (normed_in * gain_rows[0]).astype(jnp.bfloat16)
    linear = jnp.dot(normed, qkv_full, preferred_element_type=jnp.float32)
    query_rows = rotate(linear[..., :width].reshape(head_shape), cosine, sine_part).astype(
        jnp.bfloat16
    )
    key_local = rotate(
        linear[..., width : 2 * width].reshape(head_shape), cosine, sine_part
    ).astype(jnp.bfloat16)
    value_local = linear[..., 2 * width :].reshape(head_shape).astype(jnp.bfloat16)
    key_sent, value_sent = (
        lax.all_gather(key_local.reshape(fold_shape), "cp", axis=2, tiled=True),
        lax.all_gather(value_local.reshape(fold_shape), "cp", axis=2, tiled=True),
    )
    key_rows = key_sent.reshape(full_shape)
    value_rows = value_sent.reshape(full_shape)
    block_size = min(512, row_len)
    block_count = row_len // block_size
    block_range = jnp.arange(block_count)

    def block_scores(block_index):
        first_key = block_index * block_size
        key_block = lax.dynamic_slice_in_dim(key_rows, first_key, block_size, 1)
        pos_block = lax.dynamic_slice_in_dim(key_pos, first_key, block_size, 0)
        start_block = lax.dynamic_slice_in_dim(key_start, first_key, block_size, 1)
        raw_scores = jnp.einsum(
            "rqhd,rkhd->rhqk", query_rows, key_block, preferred_element_type=jnp.float32
        )
        allowed = (query_start[:, None, :, None] == start_block[:, None, None, :]) & (
            pos_block[None, None, None, :] <= query_pos[None, None, :, None]
        )
        return (raw_scores * score_scale, allowed)

    def max_step(carry, block_index):
        running_max, running_sum = carry
        scores, allowed = block_scores(block_index)
        scores = jnp.where(allowed, scores, MASKED)
        new_max = jnp.maximum(running_max, jnp.max(scores, axis=-1))
        running_sum = running_sum * jnp.exp(running_max - new_max) + jnp.sum(
            jnp.where(allowed, jnp.exp(scores - new_max[..., None]), 0.0), axis=-1
        )
        return ((new_max, running_sum), None)

    stat_shape = (row_count, HEADS, queries_dev)
    (running_max, running_sum), _ = lax.scan(
        max_step,
        (jnp.full(stat_shape, MASKED, jnp.float32), jnp.zeros(stat_shape, jnp.float32)),
        block_range,
    )
    log_total = running_max + jnp.log(running_sum)

    def value_step(totals, block_index):
        scores, allowed = block_scores(block_index)
        probs = jnp.where(allowed, jnp.exp(scores - log_total[..., None]), 0.0).astype(jnp.bfloat16)
        value_block = lax.dynamic_slice_in_dim(value_rows, block_index * block_size, block_size, 1)
        return (
            totals
            + jnp.einsum("rhqk,rkhd->rqhd", probs, value_block, preferred_element_type=jnp.float32),
            None,
        )

    attended, _ = lax.scan(value_step, jnp.zeros(head_shape, jnp.float32), block_range)
    mixed_heads = attended.reshape(flat_shape).astype(jnp.bfloat16)
    branch = jnp.dot(mixed_heads, out_full, preferred_element_type=jnp.float32)
    branch_hat = layer_norm(branch)
    hidden = inputs + branch_hat * gain_rows[1]
    hidden_hat = layer_norm(hidden)
    normed_mid = (hidden_hat * gain_rows[2]).astype(jnp.bfloat16)
    ffn_in = lax.all_gather(normed_mid.reshape(fold_shape), "cp", axis=2, tiled=True).reshape(
        group_total, width
    )
    up_proj = jnp.dot(ffn_in, up_rows, preferred_element_type=jnp.float32)
    activation = gelu_tanh(up_proj).astype(jnp.bfloat16)
    down_terms = jnp.dot(activation, down_rows, preferred_element_type=jnp.float32)
    down_proj = (
        lax.psum_scatter(
            down_terms.reshape(group_shape).astype(jnp.bfloat16),
            "cp",
            scatter_dimension=2,
            tiled=True,
        )
        .astype(jnp.float32)
        .reshape(flat_shape)
    )
    down_hat = layer_norm(down_proj)
    mixed = (hidden + down_hat * gain_rows[3]).astype(jnp.bfloat16).reshape(tokens.shape)
    upstream = cotangent.astype(jnp.float32).reshape(flat_shape)
    gain_four = jnp.sum(upstream * down_hat, axis=(0, 1))
    grad_down_out = norm_back(down_proj, upstream * gain_rows[3]).astype(jnp.bfloat16)
    grad_out_rows = lax.all_gather(
        grad_down_out.reshape(fold_shape), "cp", axis=2, tiled=True
    ).reshape(group_total, width)
    down_local = jnp.einsum(
        "tf,td->fd", activation, grad_out_rows, preferred_element_type=jnp.float32
    )
    grad_act = jnp.einsum("td,fd->tf", grad_out_rows, down_rows, preferred_element_type=jnp.float32)
    _, gelu_pull = jax.vjp(gelu_tanh, up_proj)
    grad_up = gelu_pull(grad_act)[0].astype(jnp.bfloat16)
    up_local = jnp.einsum("tc,tf->cf", ffn_in, grad_up, preferred_element_type=jnp.float32)
    mid_terms = jnp.einsum("tf,cf->tc", grad_up, up_rows, preferred_element_type=jnp.float32)
    grad_mid = (
        lax.psum_scatter(
            mid_terms.reshape(group_shape).astype(jnp.bfloat16),
            "cp",
            scatter_dimension=2,
            tiled=True,
        )
        .astype(jnp.float32)
        .reshape(flat_shape)
    )
    gain_three = jnp.sum(grad_mid * hidden_hat, axis=(0, 1))
    grad_hidden = upstream + norm_back(hidden, grad_mid * gain_rows[2])
    gain_two = jnp.sum(grad_hidden * branch_hat, axis=(0, 1))
    grad_branch = norm_back(branch, grad_hidden * gain_rows[1]).astype(jnp.bfloat16)
    out_local = jnp.einsum(
        "tc,te->ce",
        mixed_heads.reshape(token_total, width),
        grad_branch.reshape(token_total, width),
        preferred_element_type=jnp.float32,
    )
    grad_heads = (
        jnp.einsum("rqe,ce->rqc", grad_branch, out_full, preferred_element_type=jnp.float32)
        .astype(jnp.bfloat16)
        .reshape(head_shape)
    )
    delta_sum = jnp.transpose(
        jnp.sum(grad_heads.astype(jnp.float32) * attended, axis=-1), (0, 2, 1)
    )

    def score_grads(block_index):
        scores, allowed = block_scores(block_index)
        probs = jnp.where(allowed, jnp.exp(scores - log_total[..., None]), 0.0)
        first_key = block_index * block_size
        key_block = lax.dynamic_slice_in_dim(key_rows, first_key, block_size, 1)
        value_block = lax.dynamic_slice_in_dim(value_rows, first_key, block_size, 1)
        grad_probs = jnp.einsum(
            "rqhd,rkhd->rhqk", grad_heads, value_block, preferred_element_type=jnp.float32
        )
        grad_scores = (probs * (grad_probs - delta_sum[..., None]) * score_scale).astype(
            jnp.bfloat16
        )
        return (probs, grad_scores, key_block)

    def grad_step(grad_query, block_index):
        probs, grad_scores, key_block = score_grads(block_index)
        grad_query = grad_query + jnp.einsum(
            "rhqk,rkhd->rqhd", grad_scores, key_block, preferred_element_type=jnp.float32
        )
        key_part = jnp.einsum(
            "rhqk,rqhd->rkhd", grad_scores, query_rows, preferred_element_type=jnp.float32
        )
        value_part = jnp.einsum(
            "rhqk,rqhd->rkhd",
            probs.astype(jnp.bfloat16),
            grad_heads,
            preferred_element_type=jnp.float32,
        )
        return (grad_query, (key_part, value_part))

    grad_query, (key_parts, value_parts) = lax.scan(
        grad_step, jnp.zeros(head_shape, jnp.float32), block_range
    )
    key_terms = jnp.moveaxis(key_parts, 0, 1).reshape(group_shape)
    value_terms = jnp.moveaxis(value_parts, 0, 1).reshape(group_shape)
    key_sum, value_sum = (
        lax.psum_scatter(
            key_terms.astype(jnp.bfloat16), "cp", scatter_dimension=2, tiled=True
        ).astype(jnp.float32),
        lax.psum_scatter(
            value_terms.astype(jnp.bfloat16), "cp", scatter_dimension=2, tiled=True
        ).astype(jnp.float32),
    )
    query_unturned = rotate(rounded(grad_query), cosine, -sine_part).reshape(flat_shape)
    key_unturned = rotate(rounded(key_sum.reshape(head_shape)), cosine, -sine_part).reshape(
        flat_shape
    )
    grad_linear = jnp.concatenate(
        [query_unturned, key_unturned, value_sum.reshape(flat_shape)], axis=-1
    ).astype(jnp.bfloat16)
    qkv_local = jnp.einsum(
        "tc,te->ce",
        normed.reshape(token_total, width),
        grad_linear.reshape(token_total, 3 * width),
        preferred_element_type=jnp.float32,
    )
    grad_normed = jnp.einsum(
        "rqe,ce->rqc", grad_linear, qkv_full, preferred_element_type=jnp.float32
    )
    gain_one = jnp.sum(grad_normed * normed_in, axis=(0, 1))
    tokens_grad = (grad_hidden + norm_back(inputs, grad_normed * gain_rows[0])).reshape(
        tokens.shape
    )
    gain_local = jnp.concatenate([gain_one, gain_two, gain_three, gain_four])
    gain_order = jnp.transpose(gain_local.reshape(rows_count, cp_count, -1), (1, 0, 2)).reshape(-1)
    qkv_mid, out_mid, gain_mid = (
        lax.psum_scatter(
            qkv_local.astype(jnp.bfloat16), "cp", scatter_dimension=1, tiled=True
        ).astype(jnp.float32),
        lax.psum_scatter(
            out_local.astype(jnp.bfloat16), "cp", scatter_dimension=1, tiled=True
        ).astype(jnp.float32),
        lax.psum_scatter(
            gain_order.astype(jnp.bfloat16), "cp", scatter_dimension=0, tiled=True
        ).astype(jnp.float32),
    )
    qkv_sum, out_sum, up_sum, down_sum, gain_sum = (
        lax.psum_scatter(
            qkv_mid.astype(jnp.bfloat16), "rows", scatter_dimension=0, tiled=True
        ).astype(jnp.float32),
        lax.psum_scatter(
            out_mid.astype(jnp.bfloat16), "rows", scatter_dimension=0, tiled=True
        ).astype(jnp.float32),
        lax.psum_scatter(
            up_local.astype(jnp.bfloat16), "rows", scatter_dimension=0, tiled=True
        ).astype(jnp.float32),
        lax.psum_scatter(
            down_local.astype(jnp.bfloat16), "rows", scatter_dimension=1, tiled=True
        ).astype(jnp.float32),
        lax.psum_scatter(
            gain_mid.astype(jnp.bfloat16), "rows", scatter_dimension=0, tiled=True
        ).astype(jnp.float32),
    )
    return (mixed, tokens_grad, qkv_sum, out_sum, up_sum, down_sum, gain_sum)


F32 = jnp.float32
BF16 = jnp.bfloat16
MIB = 1024 * 1024


def params(grid_rank, mebibytes=24):
    return pltpu.CompilerParams(
        dimension_semantics=("arbitrary",) * grid_rank, vmem_limit_bytes=mebibytes * MIB
    )


def lasting(microseconds):
    return pl.CostEstimate(
        flops=int(microseconds * 1e7), bytes_accessed=1024, transcendentals=0
    )


def turned(x, cosine, sine):
    lane = lax.broadcasted_iota(jnp.int32, x.shape, 1)
    other = jnp.where((lane & 32) == 0, pltpu.roll(x, 96, 1), pltpu.roll(x, 32, 1))
    return x * cosine + other * sine


def attend_kernel(tile, bounds, slot_of, q_ref, k_ref, v_ref, pcol_ref, prow_ref, srow_ref,
                  o_ref, ob_ref, lse_ref, vt_ref):
    i = pl.program_id(1)

    @pl.when(i == 0)
    def _():
        vt_ref[...] = v_ref[...].astype(F32).T.astype(BF16)

    qt = q_ref[...].astype(F32).T
    row = lax.broadcasted_iota(jnp.int32, qt.shape, 0)
    lo = bounds[0, i]
    mid = jnp.minimum(bounds[1, i], i)
    qpos = prow_ref[...]
    qstart = srow_ref[...]
    qh = [jnp.where((row >= 64) == (h == 1), qt, 0.0).astype(BF16) for h in range(2)]

    def step(j, carry, masked):
        at = pl.multiple_of(j * tile, tile)
        k = k_ref[pl.ds(at, tile), :]
        scores = [jnp.dot(k, qh[h], preferred_element_type=F32) for h in range(2)]
        if masked:
            kpos = pcol_ref[pl.ds(at, tile), :]
            allowed = (kpos >= qstart) & (kpos <= qpos)
            scores = [jnp.where(allowed, s, MASKED) for s in scores]
        out = []
        for h in range(2):
            top, total, acc = carry[h]
            new = jnp.maximum(top, jnp.max(scores[h], axis=0, keepdims=True))
            p = jnp.exp(scores[h] - new)
            keep = jnp.exp(top - new)
            total = total * keep + jnp.sum(p, axis=0, keepdims=True)
            acc = acc * keep + jnp.dot(
                vt_ref[h * 64 : h * 64 + 64, pl.ds(at, tile)], p.astype(BF16),
                preferred_element_type=F32,
            )
            out.append((new, total, acc))
        return tuple(out)

    start = (
        jnp.full((1, tile), MASKED, F32), jnp.zeros((1, tile), F32), jnp.zeros((64, tile), F32)
    )
    carry = step(i, (start, start), True)
    carry = lax.fori_loop(lo, mid, functools.partial(step, masked=True), carry)
    carry = lax.fori_loop(mid, i, functools.partial(step, masked=False), carry)
    parts = []
    for h in range(2):
        top, total, acc = carry[h]
        lse_ref[0, h : h + 1, :] = top + jnp.log(total)
        parts.append(acc / total)
    out = jnp.concatenate(parts, axis=0).T
    o_ref[...] = out
    span = ob_ref.shape[1]
    for b in range(tile // span):
        ob_ref[slot_of[i * (tile // span) + b]] = out[b * span : (b + 1) * span].astype(BF16)


def attend(pair, q, k, v, pcol, prow, srow, bounds, slot_of, tile):
    rows, width = q.shape
    blocks = slot_of.shape[0]
    span = rows // blocks
    count = rows // tile
    grid_spec = pltpu.PrefetchScalarGridSpec(
        num_scalar_prefetch=2,
        grid=(1, count),
        in_specs=[
            pl.BlockSpec((tile, 128), lambda p, i, b, t: (i, pair)),
            pl.BlockSpec((rows, 128), lambda p, i, b, t: (0, pair)),
            pl.BlockSpec((rows, 128), lambda p, i, b, t: (0, pair)),
            pl.BlockSpec((rows, 1), lambda p, i, b, t: (0, 0)),
            pl.BlockSpec((1, tile), lambda p, i, b, t: (0, i)),
            pl.BlockSpec((1, tile), lambda p, i, b, t: (0, i)),
        ],
        out_specs=[
            pl.BlockSpec((tile, 128), lambda p, i, b, t: (i, p)),
            pl.BlockSpec((blocks, span, 128), lambda p, i, b, t: (0, 0, p)),
            pl.BlockSpec((1, 2, tile), lambda p, i, b, t: (p, 0, i)),
        ],
        scratch_shapes=[pltpu.VMEM((128, rows), BF16)],
    )
    return pl.pallas_call(
        functools.partial(attend_kernel, tile),
        grid_spec=grid_spec,
        out_shape=[
            jax.ShapeDtypeStruct((rows, 128), F32),
            jax.ShapeDtypeStruct((blocks, span, 128), BF16),
            jax.ShapeDtypeStruct((1, 2, rows), F32),
        ],
        compiler_params=params(2),
        cost_estimate=lasting(14),
        name="attend",
    )(bounds, slot_of, q, k, v, pcol, prow, srow)


def attend_back_kernel(tile, first, steps, bounds, slot_of, q_ref, k_ref, v_ref, do_ref, o_ref,
                       lse_ref, pcol_ref, prow_ref, srow_ref, cos_ref, sin_ref, *refs):
    qm, dom, qtm, dotm, delta, dqt = refs[-6:]
    count = q_ref.shape[0] // tile
    last = first + steps
    before = refs[0] if first else None
    g_ref = refs[1 if first else 0]
    after_ref = refs[1] if last < count else None
    j = first + pl.program_id(1)
    span = do_ref.shape[1]

    @pl.when(pl.program_id(1) == 0)
    def _():
        for t in range(first, count):
            part = pl.ds(t * tile, tile)
            q = q_ref[part, :].astype(F32)
            do = jnp.concatenate(
                [do_ref[slot_of[t * tile // span + b]] for b in range(tile // span)], axis=0
            ).astype(F32)
            qt, dot = q.T, do.T
            lane = lax.broadcasted_iota(jnp.int32, q.shape, 1)
            row = lax.broadcasted_iota(jnp.int32, qt.shape, 0)
            prod = dot * o_ref[part, :].T
            for h in range(2):
                mine = (lane >= 64) == (h == 1)
                mine_t = (row >= 64) == (h == 1)
                qm[h, part, :] = jnp.where(mine, q, 0.0).astype(BF16)
                dom[h, part, :] = jnp.where(mine, do, 0.0).astype(BF16)
                qtm[h, :, part] = jnp.where(mine_t, qt, 0.0).astype(BF16)
                dotm[h, :, part] = jnp.where(mine_t, dot, 0.0).astype(BF16)
                delta[h : h + 1, part] = jnp.sum(
                    prod[h * 64 : h * 64 + 64], axis=0, keepdims=True
                )
        if before is None:
            dqt[...] = jnp.zeros_like(dqt)
        else:
            dqt[:, first * tile :] = before[0]

    here = pl.ds(pl.multiple_of(j * tile, tile), tile)
    k = k_ref[here, :]
    v = v_ref[here, :]
    kt = k.astype(F32).T.astype(BF16)
    kpos = pcol_ref[here, :]
    full = jnp.maximum(bounds[2, j], j + 1)
    end = bounds[3, j]

    def step(i, carry, masked):
        dk, dv = carry
        part = pl.ds(pl.multiple_of(i * tile, tile), tile)
        if masked:
            allowed = (kpos >= srow_ref[:, part]) & (kpos <= prow_ref[:, part])
        for h in range(2):
            s = jnp.dot(k, qtm[h, :, part], preferred_element_type=F32)
            p = jnp.exp(s - lse_ref[0, h : h + 1, part])
            if masked:
                p = jnp.where(allowed, p, 0.0)
            dp = jnp.dot(v, dotm[h, :, part], preferred_element_type=F32)
            ds = (p * (dp - delta[h : h + 1, part])).astype(BF16)
            dv = dv + jnp.dot(p.astype(BF16), dom[h, part, :], preferred_element_type=F32)
            dk = dk + jnp.dot(ds, qm[h, part, :], preferred_element_type=F32)
            dqt[h * 64 : h * 64 + 64, part] += jnp.dot(
                kt[h * 64 : h * 64 + 64, :], ds, preferred_element_type=F32
            )
        return dk, dv

    carry = (jnp.zeros((tile, 128), F32), jnp.zeros((tile, 128), F32))
    carry = step(j, carry, True)
    carry = lax.fori_loop(j + 1, full, functools.partial(step, masked=False), carry)
    carry = lax.fori_loop(full, end, functools.partial(step, masked=True), carry)
    dk, dv = carry

    def unturned(x, at):
        x = x.astype(BF16).astype(F32)
        return turned(x, cos_ref[at, :], -sin_ref[at, :]).astype(BF16)

    grad_k, grad_v = unturned(dk, here), dv.astype(BF16)
    for b in range(tile // span):
        at = slot_of[j * (tile // span) + b] >> 1
        g_ref[at, :, 128:256] = grad_k[b * span : (b + 1) * span]
        g_ref[at, :, 256:384] = grad_v[b * span : (b + 1) * span]

    @pl.when(pl.program_id(1) == steps - 1)
    def _():
        for t in range(first, last):
            part = pl.ds(t * tile, tile)
            grad_q = unturned(dqt[:, part].T * 0.125, part)
            for b in range(tile // span):
                at = slot_of[t * (tile // span) + b] >> 1
                g_ref[at, :, 0:128] = grad_q[b * span : (b + 1) * span]
        if after_ref is not None:
            after_ref[0] = dqt[:, last * tile :]


def attend_back(half, q, k, v, do, o, lse, pcol, prow, srow, cosine, sine, bounds, slot_of, tile,
                before):
    rows, width = q.shape
    pairs = width // 128
    blocks, span, _ = do.shape
    count = rows // tile
    steps = count // 2
    first = half * steps
    whole = pl.BlockSpec((rows, 128), lambda p, j, b, t: (0, p))
    table = pl.BlockSpec((rows, 128), lambda p, j, b, t: (0, 0))
    line = pl.BlockSpec((1, rows), lambda p, j, b, t: (0, 0))
    rest = pl.BlockSpec((1, 128, rows // 2), lambda p, j, b, t: (p, 0, 0))
    outs = [
        (
            jax.ShapeDtypeStruct((blocks // 2, span, 3 * width), BF16),
            pl.BlockSpec((blocks // 2, span, 384), lambda p, j, b, t: (0, 0, p)),
        )
    ]
    if not half:
        outs.append((jax.ShapeDtypeStruct((pairs, 128, rows // 2), F32), rest))
    grid_spec = pltpu.PrefetchScalarGridSpec(
        num_scalar_prefetch=2,
        grid=(pairs, steps),
        in_specs=[
            whole, whole, whole,
            pl.BlockSpec((blocks, span, 128), lambda p, j, b, t: (0, 0, p)),
            whole,
            pl.BlockSpec((1, 2, rows), lambda p, j, b, t: (p, 0, 0)),
            pl.BlockSpec((rows, 1), lambda p, j, b, t: (0, 0)),
            line, line, table, table,
        ]
        + [rest] * len(before),
        out_specs=[spec for _, spec in outs],
        scratch_shapes=[
            pltpu.VMEM((2, rows, 128), BF16), pltpu.VMEM((2, rows, 128), BF16),
            pltpu.VMEM((2, 128, rows), BF16), pltpu.VMEM((2, 128, rows), BF16),
            pltpu.VMEM((2, rows), F32), pltpu.VMEM((128, rows), F32),
        ],
    )
    return pl.pallas_call(
        functools.partial(attend_back_kernel, tile, first, steps),
        grid_spec=grid_spec,
        out_shape=[shape for shape, _ in outs],
        compiler_params=params(2, 40),
        cost_estimate=lasting(23),
        name="attend_back",
    )(bounds, slot_of, q, k, v, do, o, lse, pcol, prow, srow, cosine, sine, *before)


def tile_bounds(starts_nat, tile):
    rows = starts_nat.shape[0]
    count = rows // tile
    tiles = starts_nat.reshape(count, tile)
    first, last = tiles[:, 0], tiles[:, -1]
    at = jnp.arange(count, dtype=jnp.int32) * tile
    lo = first // tile
    mid = (last + tile - 1) // tile
    full = jnp.sum((last[None, :] <= at[:, None]).astype(jnp.int32), axis=1)
    end = jnp.sum((first[None, :] <= at[:, None] + tile - 1).astype(jnp.int32), axis=1)
    return jnp.stack([lo, mid, full, end]).astype(jnp.int32)


def normalized(x):
    centred = x - jnp.mean(x, axis=1, keepdims=True)
    scale = lax.rsqrt(jnp.mean(centred * centred, axis=1, keepdims=True) + NORM_EPS)
    return centred * scale, scale


def normalized_back(hat, scale, upstream):
    level = jnp.mean(upstream, axis=1, keepdims=True)
    slant = jnp.mean(upstream * hat, axis=1, keepdims=True)
    return scale * (upstream - level - hat * slant)


def dot_nt(a, b):
    return lax.dot_general(a, b, (((1,), (1,)), ((), ())), preferred_element_type=F32)


def call(kernel, name, grid, tables, ins, outs, microseconds, *arrays):
    return pl.pallas_call(
        kernel,
        grid_spec=pltpu.PrefetchScalarGridSpec(
            num_scalar_prefetch=len(tables),
            grid=grid,
            in_specs=ins,
            out_specs=[spec for _, spec in outs],
        ),
        out_shape=[shape for shape, _ in outs],
        compiler_params=params(len(grid)),
        cost_estimate=lasting(microseconds),
        name=name,
    )(*tables, *arrays)


def shaped(dtype, *shape):
    return jax.ShapeDtypeStruct(shape, dtype)


def fixed(*shape):
    return pl.BlockSpec(shape, lambda *_: (0,) * len(shape))


def project_kernel(blocks, slots, near, far, gain_ref, w_ref, cos_ref, sin_ref, *refs):
    q_ref, k_ref, v_ref, n_ref = refs[-4:]
    width = q_ref.shape[1]
    x = jnp.where(slots[pl.program_id(0)] < 4, near[0], far[0]).astype(F32)
    normed = (normalized(x)[0] * gain_ref[0:1, :]).astype(BF16)
    n_ref[0] = normed
    linear = jnp.dot(normed, w_ref[...], preferred_element_type=F32)
    for at in range(0, width, 128):
        q = turned(linear[:, 3 * at : 3 * at + 128], cos_ref[...], sin_ref[...])
        k = turned(linear[:, 3 * at + 128 : 3 * at + 256], cos_ref[...], sin_ref[...])
        q_ref[:, at : at + 128] = q.astype(BF16) * jnp.asarray(0.125, BF16)
        k_ref[:, at : at + 128] = k.astype(BF16)
        v_ref[:, at : at + 128] = linear[:, 3 * at + 256 : 3 * at + 384].astype(BF16)


def project(near, far, gains, w, cosine, sine, blocks, slots, before):
    _, rows, depth = near.shape
    width = w.shape[1] // 3
    count = 2 * blocks.shape[0]
    piece = pl.BlockSpec((1, rows, depth), lambda i, b, s: (s[i] & 1, 0, 0))
    angle = pl.BlockSpec((rows, 128), lambda i, b, s: (b[i], 0))
    out = shaped(BF16, count * rows, width)
    normed = shaped(BF16, count, rows, depth)
    block = pl.BlockSpec((rows, width), lambda i, b, s: (b[i], 0))
    return pl.pallas_call(
        project_kernel,
        grid_spec=pltpu.PrefetchScalarGridSpec(
            num_scalar_prefetch=2,
            grid=blocks.shape,
            in_specs=[piece, piece, fixed(*gains.shape), fixed(*w.shape), angle, angle]
            + [pl.BlockSpec(memory_space=pl.ANY)] * len(before),
            out_specs=[
                block, block, block,
                pl.BlockSpec((1, rows, depth), lambda i, b, s: ((s[i] & 1) * 4 + (s[i] >> 1), 0, 0)),
            ],
        ),
        out_shape=[out, out, out, normed],
        input_output_aliases={8 + n: n for n in range(len(before))},
        compiler_params=params(1),
        cost_estimate=lasting(7),
        name="project",
    )(blocks, slots, near, far, gains, w, cosine, sine, *before)


def mix_kernel(group, own, near, far, both, w_ref, x_ref, gain_ref,
               heads_ref, hat_ref, scale_ref, hidden_ref, mid_ref):
    width = own.shape[2]
    for r, piece in enumerate((own[0], far[0], near[0], both[0])):
        at = pl.ds(pl.multiple_of((group[0] ^ r) * width, width), width)
        heads_ref[:, at] = piece
    branch = jnp.dot(heads_ref[...], w_ref[...], preferred_element_type=F32)
    hat, scale = normalized(branch)
    hidden = x_ref[0].astype(F32) + hat * gain_ref[1:2, :]
    hat_ref[...] = hat
    scale_ref[...] = scale
    hidden_ref[...] = hidden
    mid_ref[...] = (normalized(hidden)[0] * gain_ref[2:3, :]).astype(BF16)


def mix(group, local, near, far, both, w, x, gains):
    _, rows, part = local.shape
    count, _, width = x.shape
    block = pl.BlockSpec((1, rows, part), lambda i, g: (i, 0, 0))
    row = pl.BlockSpec((rows, width), lambda i, g: (i, 0))
    total = count * rows
    return call(
        mix_kernel, "mix", (count,), [group],
        [
            block, block, block, block, fixed(*w.shape), pl.BlockSpec((1, rows, width), lambda i, g: (i, 0, 0)),
            fixed(*gains.shape),
        ],
        [
            (shaped(BF16, total, width), row),
            (shaped(F32, total, width), row),
            (shaped(F32, total, 1), pl.BlockSpec((rows, 1), lambda i, g: (i, 0))),
            (shaped(F32, total, width), row),
            (shaped(BF16, total, width), row),
        ],
        6, local, near, far, both, w, x, gains,
    )


def finish_kernel(terms_ref, sent_ref, hidden_ref, dy_ref, gain_ref, mixed_ref, grad_ref, sum_ref):
    down = terms_ref[...] + sent_ref[...].astype(F32)
    hat, scale = normalized(down)
    gain = gain_ref[3:4, :]
    dy = dy_ref[...].astype(F32)
    mixed_ref[...] = (hidden_ref[...] + hat * gain).astype(BF16)
    grad_ref[...] = normalized_back(hat, scale, dy * gain).astype(BF16)

    @pl.when(pl.program_id(0) == 0)
    def _():
        sum_ref[...] = jnp.zeros_like(sum_ref)

    sum_ref[...] += jnp.sum(dy * hat, axis=0, keepdims=True)


def finish(terms, sent, hidden, dy, gains):
    total, width = terms.shape
    rows = total // 2
    row = pl.BlockSpec((rows, width), lambda i: (i, 0))
    return call(
        finish_kernel, "finish", (2,), [],
        [row, row, row, row, fixed(*gains.shape)],
        [
            (shaped(BF16, total, width), row), (shaped(BF16, total, width), row),
            (shaped(F32, 1, width), fixed(1, width)),
        ],
        5, terms, sent, hidden, dy, gains,
    )


def turn_kernel(group, terms_ref, sent_ref, hidden_ref, dy_ref, hat_ref, scale_ref, w_ref, gain_ref,
                keep_ref, branch_ref, heads_ref, three_ref, two_ref):
    upstream = terms_ref[...] + sent_ref[...].astype(F32)
    hat, scale = normalized(hidden_ref[...])

    @pl.when(pl.program_id(0) == 0)
    def _():
        three_ref[...] = jnp.zeros_like(three_ref)
        two_ref[...] = jnp.zeros_like(two_ref)

    three_ref[...] += jnp.sum(upstream * hat, axis=0, keepdims=True)
    grad = dy_ref[...].astype(F32) + normalized_back(hat, scale, upstream * gain_ref[2:3, :])
    keep_ref[...] = grad
    branch_hat = hat_ref[...]
    two_ref[...] += jnp.sum(grad * branch_hat, axis=0, keepdims=True)
    branch = normalized_back(branch_hat, scale_ref[...], grad * gain_ref[1:2, :]).astype(BF16)
    branch_ref[...] = branch
    part = heads_ref.shape[3]
    for r in range(4):
        at = pl.ds(pl.multiple_of((group[0] ^ r) * part, part), part)
        heads_ref[r, 0] = dot_nt(branch, w_ref[at, :]).astype(BF16)


def turn(group, terms, sent, hidden, dy, hat, scale, w, gains):
    total, width = terms.shape
    rows = total // 2
    part = width // 4
    row = pl.BlockSpec((rows, width), lambda i, g: (i, 0))
    return call(
        turn_kernel, "turn", (2,), [group],
        [
            row, row, row, row, row, pl.BlockSpec((rows, 1), lambda i, g: (i, 0)),
            fixed(*w.shape), fixed(*gains.shape),
        ],
        [
            (shaped(F32, total, width), row), (shaped(BF16, total, width), row),
            (
                shaped(BF16, 4, 2, rows, part),
                pl.BlockSpec((4, 1, rows, part), lambda i, g: (0, i, 0, 0)),
            ),
            (shaped(F32, 1, width), fixed(1, width)), (shaped(F32, 1, width), fixed(1, width)),
        ],
        8, terms, sent, hidden, dy, hat, scale, w, gains,
    )


def end_kernel(keep_ref, far_ref, x_ref, grad_ref, gain_ref, o_ref):
    upstream = keep_ref[...] + far_ref[...].astype(F32)
    hat, scale = normalized(x_ref[...].astype(F32))
    grad = grad_ref[...] + normalized_back(hat, scale, upstream * gain_ref[0:1, :])
    o_ref[...] = grad.astype(BF16)


def end(keep, far, x, grad, gains):
    total, width = x.shape
    rows = total // 2
    row = pl.BlockSpec((rows, width), lambda i: (i, 0))
    return call(
        end_kernel, "end", (2,), [], [row] * 4 + [fixed(*gains.shape)],
        [(shaped(BF16, total, width), row)], 20, keep, far, x, grad, gains,
    )[0]


def plain(x):
    return with_layout_constraint(x, Layout(tuple(range(x.ndim))))


def cut_lines_kernel(place, *refs):
    for n, out in enumerate(refs[8:]):
        up, down = refs[2 * n], refs[2 * n + 1]
        lines = up.shape[0]
        out[0, :lines] = up[...]
        out[0, lines:] = down[: out.shape[1] - lines]


def cut_lines(place, up, down, spare):
    width = up.shape[1]
    lines = up.shape[0] // 8
    at = (
        lambda i, p: (2 * (2 * i + p[0]), 0),
        lambda i, p: (2 * (2 * i + 1 - p[0]), 0),
        lambda i, p: (2 * (2 * p[1] + i) + 1, 0),
        lambda i, p: (2 * (2 * (1 - p[1]) + i) + 1, 0),
    )
    rows = 2 * lines - spare
    out = shaped(BF16, 2, rows, width), pl.BlockSpec((1, rows, width), lambda i, p: (i, 0, 0))
    return call(
        cut_lines_kernel, "cut_lines", (2,), [place],
        [pl.BlockSpec((lines, width), index) for index in at for _ in range(2)],
        [out] * 4, 4, *([up, down] * 4),
    )


QKV_BLOCKS, OVER_BLOCKS, OUT_BLOCKS = 12, 2, 8
LOW_BLOCKS = 11
ALL_BLOCKS = QKV_BLOCKS + OVER_BLOCKS + OUT_BLOCKS + 1
LEFT = ((0, 0), (0, 1), (1, 0))
RIGHT = ((1, 1), (2, 0), (2, 1))


def tiles(array):
    return [array[:, at : at + 128] for at in range(0, array.shape[1], 128)]


def plus(a, b):
    return (a.astype(F32) + b.astype(F32)).astype(BF16)


def spread_first_kernel(place, qkv_ref, out_ref, gain_ref, over_ref, far_ref, out_far,
                        low, low_away, high, high_away):
    lines = far_ref.shape[1]
    spare = over_ref.shape[0] // 8
    wide = qkv_ref.shape[1]
    x_bit, y_bit, core = place[0], place[1], place[2]

    def fill(line, low_out, high_out):
        at = pl.ds(pl.multiple_of((2 * line + core) * lines, lines), lines)
        near = tiles(qkv_ref[at, :])
        far = tiles(far_ref[line, :, :wide])
        blocks = [jnp.where(core == 0, a, b) for a, b in zip(near, far)]
        blocks += [jnp.where(core == 0, a, b) for a, b in zip(far, near)]
        for c in range(2):
            rows = pl.ds(pl.multiple_of((2 * line + c) * spare, spare), spare)
            blocks.append(jnp.concatenate(tiles(over_ref[rows, :]), axis=0))
        blocks += [
            plus(a, b)
            for a, b in zip(tiles(out_ref[at, :]), tiles(out_far[line]))
        ]
        count = gain_ref.shape[1]
        gain = jnp.concatenate(
            [gain_ref[2 * line + core], jnp.zeros((lines - count, 128), BF16)], axis=0
        )
        blocks.append(plus(gain, far_ref[line, :, -128:]))
        for n, block in enumerate(blocks):
            if n < LOW_BLOCKS and low_out is not None:
                low_out[n] = block
            if n >= LOW_BLOCKS and high_out is not None:
                high_out[n - LOW_BLOCKS] = block

    for n in range(2):
        fill(2 * n + x_bit, low.at[n], None)
        fill(2 * n + 1 - x_bit, low_away.at[n], None)
        fill(2 * y_bit + n, None, high.at[n])
        fill(2 * (1 - y_bit) + n, None, high_away.at[n])


def spread_first(place, qkv, out, gain, over, far, out_far):
    lines = far.shape[1]
    low = shaped(BF16, 2, LOW_BLOCKS, lines, 128), fixed(2, LOW_BLOCKS, lines, 128)
    rest = ALL_BLOCKS - LOW_BLOCKS
    high = shaped(BF16, 2, rest, lines, 128), fixed(2, rest, lines, 128)
    arrays = (qkv, out, gain, over, far, out_far)
    return call(
        spread_first_kernel, "spread_first", (1,), [place], [fixed(*a.shape) for a in arrays],
        [low, low, high, high], 2, *arrays,
    )


def spread_second_kernel(place, low, low_far, high, high_far, low_o, low_away, high_o, high_away):
    for source, far, bit, near_o, away_o in (
        (low, low_far, place[1], low_o, low_away), (high, high_far, place[0], high_o, high_away)
    ):
        near_o[...] = plus(source[bit], far[bit])
        away_o[...] = plus(source[1 - bit], far[1 - bit])


def spread_second(place, *arrays):
    lows, highs = arrays[0].shape[1:], arrays[2].shape[1:]
    outs = [(shaped(BF16, *s), fixed(*s)) for s in (lows, lows, highs, highs)]
    return call(
        spread_second_kernel, "spread_second", (1,), [place], [fixed(*a.shape) for a in arrays],
        outs, 2, *arrays,
    )


def spread_third_kernel(place, low, low_far, high, high_far, near_o, away_o, over_o):
    half = place[4]

    def block(n):
        if n < LOW_BLOCKS:
            return plus(low[n], low_far[n])
        return plus(high[n - LOW_BLOCKS], high_far[n - LOW_BLOCKS])

    at = 0
    for (left_t, left_c), (right_t, right_c) in zip(LEFT, RIGHT):
        for pair in range(2):
            left = block(left_c * 6 + pair * 3 + left_t)
            right = block(right_c * 6 + pair * 3 + right_t)
            near_o[at] = jnp.where(half == 0, left, right)
            away_o[at] = jnp.where(half == 0, right, left)
            at += 1
    for c in range(2):
        over_o[c] = block(QKV_BLOCKS + c)
    first = QKV_BLOCKS + OVER_BLOCKS
    for n in range(4):
        left, right = block(first + n), block(first + 4 + n)
        near_o[at] = jnp.where(half == 0, left, right)
        away_o[at] = jnp.where(half == 0, right, left)
        at += 1
    near_o[at] = block(first + 8)
    away_o[at] = block(first + 8)


def spread_third(place, *arrays):
    lines = arrays[0].shape[1]
    part = shaped(BF16, 11, lines, 128), fixed(11, lines, 128)
    over = shaped(BF16, 2, lines, 128), fixed(2, lines, 128)
    return call(
        spread_third_kernel, "spread_third", (1,), [place], [fixed(*a.shape) for a in arrays],
        [part, part, over], 2, *arrays,
    )


def spread_fourth_kernel(place, near, far, near_o, away_o):
    odd = place[3] == 1
    blocks = [plus(near[n], far[n]) for n in range(11)]
    for pair in range(2):
        one, two, three = blocks[pair], blocks[2 + pair], blocks[4 + pair]
        near_o[pair] = jnp.where(odd, two, one)
        near_o[2 + pair] = jnp.where(odd, three, two)
        away_o[pair] = jnp.where(odd, one, three)
        near_o[4 + pair] = jnp.where(odd, blocks[8 + pair], blocks[6 + pair])
        away_o[2 + pair] = jnp.where(odd, blocks[6 + pair], blocks[8 + pair])
    near_o[6] = blocks[10]
    away_o[4] = blocks[10]


def spread_fourth(place, near, far):
    lines = near.shape[1]
    return call(
        spread_fourth_kernel, "spread_fourth", (1,), [place], [fixed(*near.shape)] * 2,
        [
            (shaped(BF16, 7, lines, 128), fixed(7, lines, 128)),
            (shaped(BF16, 5, lines, 128), fixed(5, lines, 128)),
        ],
        2, near, far,
    )


def spread_fifth_kernel(place, near, far, qkv_o, out_o, gain_o, gain_all):
    for pair in range(2):
        first, second = near[pair].astype(F32), near[2 + pair].astype(F32)
        other = far[pair].astype(F32)
        at = 128 * pair
        qkv_o[:, at : at + 128] = first
        qkv_o[:, 256 + at : 384 + at] = other
        qkv_o[:, 512 + at : 640 + at] = second
        out_o[:, at : at + 128] = near[4 + pair].astype(F32) + far[2 + pair].astype(F32)
    gain_all[...] = near[6].astype(F32) + far[4].astype(F32)
    gain_o[...] = gain_all[pl.ds(2 * place[4] + place[3], 1), :]


def spread_fifth(place, near, far):
    lines = near.shape[1]
    outs = [(shaped(F32, *s), fixed(*s)) for s in ((lines, 768), (lines, 256), (1, 128))]
    return pl.pallas_call(
        spread_fifth_kernel,
        grid_spec=pltpu.PrefetchScalarGridSpec(
            num_scalar_prefetch=1,
            grid=(1,),
            in_specs=[fixed(*near.shape), fixed(*far.shape)],
            out_specs=[spec for _, spec in outs],
            scratch_shapes=[pltpu.VMEM((lines, 128), F32)],
        ),
        out_shape=[shape for shape, _ in outs],
        compiler_params=params(1),
        cost_estimate=lasting(2),
        name="spread_fifth",
    )(place, near, far)


def flip(x, axis, bit):
    return lax.ppermute(plain(x), axis, [(i, i ^ bit) for i in range(lax.axis_size(axis))])


def swap(x):
    cp = lax.axis_size("cp")
    half = cp // 2
    pairs = []
    for z in range(half):
        low, high = cp + z, z + half
        pairs += [(low, high), (high, low)]
    return lax.ppermute(plain(x), ("core", "cp"), pairs)


def settled(x, moved):
    stays = (lax.axis_index("core") == 1) == (lax.axis_index("cp") >= lax.axis_size("cp") // 2)
    return jnp.where(stays, x, moved)


def ordered(first, mine, other, axis):
    return jnp.concatenate(
        [jnp.where(first, mine, other), jnp.where(first, other, mine)], axis=axis
    )


def placed(first, mine, other, at):
    return ordered(first, jnp.expand_dims(mine, at), jnp.expand_dims(other, at), at)


def after(x, *others):
    return lax.optimization_barrier((x, *others))[0]


def all_after(group, *others):
    return lax.optimization_barrier((*group, *others))[: len(group)]


def total(a, b):
    return (a.astype(F32) + b.astype(F32)).astype(BF16)


def flip_both(x):
    cp = lax.axis_size("cp")
    return lax.ppermute(
        x, ("core", "cp"), [(c * cp + z, (1 - c) * cp + (z ^ 1)) for c in range(2) for z in range(cp)]
    )


def dot(a, b, dims):
    return lax.dot_general(a, b, ((dims[:1], dims[1:]), ((), ())), preferred_element_type=F32)


def gelu_and_slope(u):
    c = math.sqrt(2.0 / math.pi)
    square = u * u
    t = jnp.tanh(u * (c + (c * 0.044715) * square))
    half = 0.5 + 0.5 * t
    slope = half + (0.5 * u) * (1.0 - t * t) * (c + (3.0 * 0.044715 * c) * square)
    return lax.optimization_barrier(((u * half).astype(BF16), slope.astype(BF16)))


def pick(x, at, axis):
    return lax.dynamic_index_in_dim(x, at, axis, False)


def widened(z, x, other):
    first, second = jnp.where(z & 1 == 0, x, other), jnp.where(z & 1 == 0, other, x)
    half = x.shape[1] // 2
    return jnp.concatenate(
        [first[:, :half], second[:, :half], first[:, half:], second[:, half:]], axis=1
    )


def body(tokens, doc_starts, qkv_weight, out_weight, up_weight, down_weight, norm_gains, cotangent):
    xy, core, z = lax.axis_index("xy"), lax.axis_index("core"), lax.axis_index("cp")
    xy_count, cp_count = lax.axis_size("xy"), lax.axis_size("cp")
    _, _, span, width = tokens.shape
    blocks = 2 * cp_count
    row_len = blocks * span
    own = 2 * span
    parity = z & 1
    group = parity + 2 * core
    part = width // cp_count
    hidden_part = up_weight.shape[1] // 2
    lines_each = width // xy_count
    lines = lines_each // 2
    here = jnp.reshape(xy, (1,)).astype(jnp.int32)
    group_at = jnp.reshape(group, (1,)).astype(jnp.int32)

    gain_rows = jnp.zeros((16, qkv_weight.shape[1]), BF16)
    gain_rows = lax.dynamic_update_slice(gain_rows, norm_gains[None], (0, 0))
    w = jnp.concatenate([qkv_weight, gain_rows])
    w_far = flip(w, "cp", 2)

    x = settled(tokens[0], swap(after(tokens, w_far)[0]))
    w, w_far = jnp.where(z & 2 == 0, w, w_far), jnp.where(z & 2 == 0, w_far, w)
    near = [w[:, n * part : (n + 1) * part] for n in range(3)]
    near += [w_far[:, n * part : (n + 1) * part] for n in range(3)]
    even = parity == 0
    sent = jnp.concatenate([near[1], near[4]], axis=1)
    gain_near = jnp.stack([w[lines, :128], w_far[lines, :128]])
    sent = lax.dynamic_update_slice(sent, gain_near, (lines, 0))
    far = flip(sent, "cp", 1)
    up_weight, down_weight, out_weight = all_after((up_weight, down_weight, out_weight), far)
    out_far = flip(out_weight, "cp", 2)


    def half_of(which):
        up = lax.dynamic_slice_in_dim(up_weight, which * hidden_part, hidden_part, 1)
        down = lax.dynamic_slice_in_dim(down_weight, which * hidden_part, hidden_part, 0)
        return plain(jnp.stack([up, down.T]))

    ffn = ordered(core == 0, half_of(core), flip(half_of(1 - core), "core", 1), 1)

    def paired(mine, other):
        return jnp.concatenate(
            [jnp.where(z & 2 == 0, mine, other), jnp.where(z & 2 == 0, other, mine)], axis=1
        )

    gain_far = far[lines : lines + 2, :128]
    gain_near, gain_far = (
        jnp.where(even, gain_near, gain_far), jnp.where(even, gain_far, gain_near)
    )
    gain_rows = jnp.stack([gain_near[0], gain_far[0], gain_near[1], gain_far[1]])
    far = [far[:lines, n * part : (n + 1) * part] for n in range(2)]
    near = [block[:lines] for block in near]

    def by_pairs(*choices):
        picked = [jnp.where(even, a, b) for a, b in choices]
        return jnp.concatenate(
            [block[:, at : at + 128] for at in range(0, part, 128) for block in picked], axis=1
        )

    first_group = by_pairs((near[0], far[0]), (far[0], near[2]), (near[5], near[3]))
    second_group = by_pairs((near[2], near[0]), (near[3], far[1]), (far[1], near[5]))
    gain_block = jnp.zeros((16, 3 * part), BF16)
    gain_block = lax.dynamic_update_slice(gain_block, gain_rows, (0, 0))
    mine = jnp.concatenate([jnp.where(core == 0, first_group, second_group), gain_block])
    other = jnp.concatenate([jnp.where(core == 0, second_group, first_group), gain_block])

    other_starts = flip(after(doc_starts, w_far), "core", 1)
    starts = jnp.where(core == z // (cp_count // 2), doc_starts, other_starts)[0]

    block_id = jnp.arange(blocks, dtype=jnp.int32)[:, None]
    inside = jnp.arange(span, dtype=jnp.int32)[None, :]
    late = block_id >= cp_count
    positions = (block_id * span + jnp.where(late, span - 1 - inside, inside)).reshape(-1)

    def starts_at(at):
        return jnp.max(jnp.where(starts[None, :] <= at[:, None], starts[None, :], 0), axis=1)

    row_start = starts_at(positions)
    tile = min(512, row_len)
    bounds = tile_bounds(starts_at(jnp.arange(row_len, dtype=jnp.int32)), tile)
    freq = jnp.exp(
        -math.log(10000.0) * 2.0 * jnp.arange(HEAD_DIM // 2, dtype=F32) / HEAD_DIM
    )
    angles = (positions - row_start).astype(F32)[:, None] * freq
    cosine, sine = jnp.cos(angles), jnp.sin(angles)
    cosine = plain(jnp.tile(cosine, (1, 4)))
    sine = plain(jnp.tile(jnp.concatenate([-sine, sine], axis=1), (1, 2)))
    pcol, prow, srow = positions[:, None], positions[None, :], row_start[None, :]
    chunk = jnp.arange(blocks, dtype=jnp.int32)
    chunk = jnp.where(chunk < cp_count, chunk, blocks - 1 - chunk)
    slot_of = (
        2 * (2 * ((chunk >> 1) ^ core) + ((chunk & 1) ^ parity))
        + (jnp.arange(blocks) >= cp_count)
    ).astype(jnp.int32)
    slot = jnp.arange(blocks, dtype=jnp.int32)
    relative = slot >> 1
    chunk_of = 2 * ((relative >> 1) ^ core) + ((relative & 1) ^ parity)
    block_of = jnp.where(slot & 1 == 0, chunk_of, blocks - 1 - chunk_of).astype(jnp.int32)

    x = after(x, sent, cosine, sine)
    x_chip = flip(x, "cp", 1)
    x_core = flip(x, "core", 1)
    up_lines, out_w, out_far = all_after((ffn[0], out_weight, out_far), x)
    up_far = flip(up_lines, "cp", 2)
    out_w = paired(out_w, out_far)
    out_far = flip(out_w, "cp", 1)

    qkv = placed(core == 0, mine, flip(other, "core", 1), 0)
    cut = qkv.shape[2] // 2
    low, high = qkv[:, :, :cut], qkv[:, :, cut:]
    low = placed(xy & 1 == 0, low, flip(low, "xy", 1), 0)
    high = placed(xy & 2 == 0, high, flip(high, "xy", 2), 0)
    low = placed(xy & 2 == 0, low, flip(low, "xy", 2), 0)
    high = placed(xy & 1 == 0, high, flip(high, "xy", 1), 1)
    qkv = jnp.concatenate([low[:, :, :, :lines], high[:, :, :, :lines]], axis=4)
    qkv = qkv.reshape(width, 3 * part)
    gains = low[:, :, :, lines : lines + cp_count, :128]
    gains = gains.reshape(4, width).astype(F32)

    sooner, later = jnp.array([0, 1, 4, 5], jnp.int32), jnp.array([2, 3, 6, 7], jnp.int32)
    early = project(x, x_core, gains, qkv, cosine, sine, block_of[sooner], sooner, [])
    x_chip, up_far, *early = lax.optimization_barrier((x_chip, up_far, *early))
    x_both = flip(x_chip, "core", 1)
    up_lines, up_far, down_lines, out_w, out_far = all_after(
        (up_lines, up_far, ffn[1], out_w, out_far), x_chip, qkv
    )
    up_lines, out_w = paired(up_lines, up_far), widened(z, out_w, out_far)[None]
    up_far = flip(up_lines, "cp", 1)
    down_far = flip(down_lines, "cp", 2)
    out_far = flip(out_w, "xy", 1)

    def halves(x):
        return x[None, :lines], x[None, lines:]

    def send_lines(low, high):
        return flip(low, "xy", 1), flip(high, "xy", 2)

    def join_lines(low, high, low_far, high_far):
        low = ordered(xy & 1 == 0, low, low_far, 0)
        high = jnp.expand_dims(ordered(xy & 2 == 0, high, high_far, 0), 1)
        return low, high

    def send_more(low, high):
        return flip(low, "xy", 2), flip(high, "xy", 1)

    def join_all(low, high, low_far, high_far):
        low = ordered(xy & 2 == 0, low, low_far, 0)
        high = ordered(xy & 1 == 0, high, high_far, 1).reshape(low.shape)
        return jnp.stack([low, high], axis=1).reshape(width, -1)

    q, k, v, normed = project(
        x_chip, x_both, gains, qkv, cosine, sine, block_of[later], later, early
    )
    up_lines, up_far, down_lines, down_far, out_w, out_far = all_after(
        (up_lines, up_far, down_lines, down_far, out_w, out_far), q
    )
    up_lines = widened(z, up_lines, up_far)
    up_full = lax.all_gather(up_lines, "xy", axis=0, tiled=True)
    out_w = ordered(xy & 1 == 0, out_w, out_far, 0)
    out_far = flip(out_w, "xy", 2)
    down_lines = paired(down_lines, down_far)
    down_far = flip(down_lines, "cp", 1)
    q = after(q, up_lines, out_w, down_lines)
    first = attend(0, q, k, v, pcol, prow, srow, bounds, slot_of, tile)
    down_lines, down_far, out_w, out_far = all_after(
        (down_lines, down_far, out_w, out_far), first[0]
    )
    out_w = ordered(xy & 2 == 0, out_w, out_far, 0)
    down_pair = halves(widened(z, down_lines, down_far))
    down_far = send_lines(*down_pair)
    q = after(q, first[0], *down_pair, out_w)
    second = attend(1, q, k, v, pcol, prow, srow, bounds, slot_of, tile)
    attended, local, lse = zip(first, second)
    local = jnp.concatenate(local, axis=2)
    out_w, down_pair, down_far = (
        after(out_w, local), all_after(down_pair, local), all_after(down_far, local)
    )
    out_w = placed(core == 0, out_w, flip(out_w, "core", 1), 1).reshape(width, width)
    down_pair = join_lines(*down_pair, *down_far)
    down_far = send_more(*down_pair)
    heads, branch_hat, branch_scale, hidden, mid = mix(
        group_at, after(local, *down_pair)[:2], flip(local[4:6], "core", 1), flip(local[2:4], "cp", 1),
        flip_both(local[6:]), out_w, x, gains,
    )

    cotangent = cotangent.reshape(own, width)
    dy_moved = swap(after(cotangent, mid))

    ffn_in = jnp.concatenate([mid, flip(mid, "core", 1)])
    act, slope = gelu_and_slope(dot(ffn_in, up_full, (1, 0)))
    down_full = join_all(*down_pair, *all_after(down_far, act))
    sent = flip(dot(act[own:], down_full, (1, 1)).astype(BF16), "core", 1)
    terms = dot(act[:own], down_full, (1, 1))
    dy = settled(cotangent, dy_moved)
    mixed, grad_down, gain_four = finish(terms, sent, hidden, dy, gains)
    grad_down = jnp.concatenate([grad_down, flip(grad_down, "core", 1)])

    x_bit, y_bit = xy & 1, xy >> 1

    def send_first(away):
        return flip(away[0], "xy", 1), flip(away[1], "xy", 2)

    def cut_second(near, far):
        away = (
            total(pick(near[0], 1 - y_bit, 0), pick(far[0], 1 - y_bit, 0)),
            total(pick(near[1], 1 - x_bit, 0), pick(far[1], 1 - x_bit, 0)),
        )
        near = (
            total(pick(near[0], y_bit, 0), pick(far[0], y_bit, 0)),
            total(pick(near[1], x_bit, 0), pick(far[1], x_bit, 0)),
        )
        return near, away

    def send_second(away):
        return flip(away[0], "xy", 2), flip(away[1], "xy", 1)

    def cut_third(near, far):
        return split_columns(
            jnp.concatenate([total(a, b) for a, b in zip(near, far)]), hidden_part
        )

    def split_columns(sums, each):
        blocks_of = [sums[:, n * each : (n + 1) * each] for n in range(cp_count)]
        odd = jnp.stack([blocks_of[1], blocks_of[3]])
        even = jnp.stack([blocks_of[0], blocks_of[2]])
        return jnp.where(parity == 0, even, odd), jnp.where(parity == 0, odd, even)

    def cut_fourth(near, far):
        return (
            total(pick(near, z >> 1, 0), pick(far, z >> 1, 0)),
            total(pick(near, 1 - (z >> 1), 0), pick(far, 1 - (z >> 1), 0)),
        )

    down_local = plain(dot(grad_down, act, (0, 0)).astype(BF16))
    grad_up = dot(after(grad_down, down_local), down_full, (1, 0)) * slope.astype(F32)
    grad_up = grad_up.astype(BF16)
    sent = flip(dot(grad_up[own:], up_full, (1, 1)).astype(BF16), "core", 1)
    up_local = plain(dot(ffn_in, grad_up, (0, 0)).astype(BF16))
    spare = lines // 4
    place = jnp.stack([x_bit, y_bit]).astype(jnp.int32)
    low, low_away, high, high_away = cut_lines(place, up_local, down_local, spare)
    grad_near, grad_away = (low, high), (low_away, high_away)
    over_local = down_local.reshape(2 * xy_count, lines, -1)[:, lines - spare :]
    over_local = over_local.reshape(2 * xy_count * spare, -1)
    grad_far = send_first(grad_away)
    terms = dot(after(grad_up, *grad_away)[:own], up_full, (1, 1))
    grad_hidden, grad_branch, grad_heads, gain_three, gain_two = turn(
        group_at, terms, sent, hidden, dy, branch_hat, branch_scale, out_w, gains
    )

    grad_local = [
        grad_heads[0], flip(grad_heads[1], "cp", 1), flip(grad_heads[2], "core", 1),
        flip_both(grad_heads[3]),
    ]
    out_local = dot(after(heads, grad_heads), grad_branch, (0, 0)).astype(BF16)
    grad_local = plain(jnp.concatenate(grad_local))
    out_away = pick(out_local.reshape(xy_count, 2, lines, width), 1 - core, 1)
    out_away, over_local, mixed, grad_local = lax.optimization_barrier(
        (out_away, over_local, mixed, grad_local)
    )
    over_near, over_away = split_columns(over_local, hidden_part)
    over_far = flip(over_away, "cp", 1)
    mixed_moved = swap(mixed)
    grad_local = after(grad_local, over_away)

    def back_to_tokens(grads):
        two = 2 * span
        rows = grads.reshape(4 * span, 3 * part)
        send = dot(rows[two:], qkv, (1, 1)).astype(BF16)
        sent = flip(send, "core", 1)
        rows = after(rows, send)
        far_away = total(dot(rows[span:two], qkv, (1, 1)), sent[span:])
        kept = dot(after(rows, far_away)[:span], qkv, (1, 1)) + sent[:span].astype(F32)
        return send, far_away, flip(far_away, "cp", 1), kept

    tables = (pcol, prow, srow, cosine, sine, bounds, slot_of, tile)
    attended, lse = jnp.concatenate(attended, axis=1), jnp.concatenate(lse, axis=0)
    first, unfinished = attend_back(0, q, k, v, grad_local, attended, lse, *tables, [])
    first, mixed_moved, over_far, *grad_far = lax.optimization_barrier(
        (first, mixed_moved, over_far, *grad_far)
    )
    over_near, over_away = cut_fourth(over_near, over_far)
    over_far = flip(over_away, "cp", 2)
    _, far_away, far_back, kept = back_to_tokens(after(first, over_away))
    grad_near, grad_away = cut_second(grad_near, all_after(grad_far, far_away))
    grad_far = send_second(grad_away)
    out_far = flip(after(out_away, far_away), "core", 1)
    second = attend_back(
        1, q, k, v, after(grad_local, first, *grad_away, over_away, kept), attended, lse, *tables,
        [unfinished],
    )[0]
    second, over_far, out_far, *grad_far = lax.optimization_barrier(
        (second, over_far, out_far, *grad_far)
    )

    ended = end(kept, after(far_back, second), x[0], grad_hidden[:span], gains)
    moved = swap(ended)
    second = after(second, ended)
    send, far_away, far, kept = back_to_tokens(second)
    qkv_local = sum(
        dot(normed[4 * h : 4 * h + 4].reshape(4 * span, width), g.reshape(4 * span, -1), (0, 0))
        for h, g in enumerate((first, after(second, send)))
    ).astype(BF16)
    gain_one = jnp.sum(qkv_local.astype(F32) * qkv.astype(F32), axis=1) / gains[0]
    gain_sum = jnp.concatenate([gain_one[None], gain_two, gain_three, gain_four])
    gain_sum = gain_sum.reshape(2 * xy_count, cp_count, 128).astype(BF16)
    place = jnp.stack([x_bit, y_bit, core, parity, z >> 1]).astype(jnp.int32)
    locals_ = (qkv_local, out_local, gain_sum)
    rest_away = jnp.concatenate(
        [
            pick(qkv_local.reshape(xy_count, 2, lines, 3 * part), 1 - core, 1),
            jnp.pad(
                pick(gain_sum.reshape(xy_count, 2, cp_count, 128), 1 - core, 1),
                ((0, 0), (0, lines - cp_count), (0, 0)),
            ),
        ],
        axis=2,
    )
    rest_far = flip(rest_away, "core", 1)

    over = total(over_near, over_far)
    rest_far, over = all_after((rest_far, over), kept)
    low, low_away, high, high_away = spread_first(place, *locals_, over, rest_far, out_far)
    rest_far = flip(low_away, "xy", 1), flip(high_away, "xy", 2)
    low, low_away, high, high_away = spread_second(place, low, rest_far[0], high, rest_far[1])
    rest_far = flip(low_away, "xy", 2), flip(high_away, "xy", 1)
    grad_near, grad_away = cut_third(grad_near, all_after(grad_far, low_away))
    grad_far = flip(grad_away, "cp", 1)
    ended_last = end(
        kept, after(far, moved, low_away, high_away), x[1], grad_hidden[span:], gains
    )
    moved_last = swap(ended_last)
    rest_far = all_after(rest_far, moved_last)
    rest, rest_away, over = spread_third(place, low, rest_far[0], high, rest_far[1])
    grad_near, grad_away = cut_fourth(grad_near, after(grad_far, rest_away))
    grad_far = flip(grad_away, "cp", 2)
    gather_away = rest_away
    rest, rest_away = spread_fourth(place, rest, flip(rest_away, "cp", 2))
    moved_last = after(moved_last, rest_away)
    qkv_grad, out_grad, gains_grad = spread_fifth(place, rest, flip(rest_away, "cp", 1))
    gains_grad = gains_grad.reshape(-1)
    tokens_grad = jnp.stack([settled(ended, moved), settled(ended_last, moved_last)])
    tokens_grad = tokens_grad.astype(F32).reshape(tokens.shape)
    mixed = settled(after(mixed, gather_away), mixed_moved).reshape(tokens.shape)

    both = total(grad_near, after(grad_far, gather_away))
    both = plain(both).reshape(2, 2 * lines - spare, hidden_part)
    over = [
        jnp.concatenate([block[n * spare : (n + 1) * spare] for n in range(4)], axis=1)
        for block in over
    ]
    both = jnp.concatenate([both, jnp.stack(over)], axis=1).reshape(2, 2, lines, hidden_part)
    mine, other = pick(both, core, 0), flip(pick(both, 1 - core, 0), "core", 1)
    up_grad = ordered(core == 0, mine[0], other[0], 1).astype(F32)
    down_grad = ordered(core == 0, mine[1], other[1], 1).T.astype(F32)
    return mixed, tokens_grad, qkv_grad, out_grad, up_grad, down_grad, gains_grad


def solution(mesh):
    rows, cp = mesh.shape["rows"], mesh.shape["cp"]
    if (rows, cp) == (8, 4):
        grid = Mesh(mesh.devices.reshape(rows // 2, 2, cp), ("xy", "core", "cp"))
        run, lines = body, ("xy", "core")
    else:
        grid, run, lines = mesh, general_body, ("rows",)
    tokens = P(lines, None, "cp", None)
    weight, down, gains = P(lines, "cp"), P("cp", lines), P(lines + ("cp",))
    return jax.shard_map(
        run,
        mesh=grid,
        in_specs=(tokens, P(lines, None), weight, weight, weight, down, gains, tokens),
        out_specs=(tokens, tokens, weight, weight, weight, down, gains),
        check_vma=False,
    )
```

profile of v0, /device:TPU:0, one launch (start us, length us, event | category | flops | bytes accessed | tf_op | source)
XLA Modules:
  0.0 479.4 jit_solution(4591958453859565508)
XLA Ops:
  8.3 4.1 collective-permute-start
  16.5 6.0 %collective-permute-done = bf16[144,768]{1,0:T(8,128)(2,1)S(1)} collective-permute-done((bf16[144,768]{1,0:T(8,128)(2,1)S(1)}, bf16[144,768]{1,0:T(8,128)(2,1)S(1)}, u32[]{:S(2)}, u32[]{:S(2)}) %collective-permute-start) | collective-permute-done | bytes 221216 | tf_op jit(solution)/shard_map/ppermute | solution.py:1020
  30.4 3.1 collective-permute-done.4
  35.6 7.0 %collective-permute-start.9 = (bf16[144,768]{1,0:T(8,128)(2,1)S(1)}, bf16[144,768]{1,0:T(8,128)(2,1)S(1)}, u32[]{:S(2)}, u32[]{:S(2)}) collective-permute-start(bf16[144,768]{1,0:T(8,128)(2,1)S(1)} %pad_maximum_fusion.21), channel_id=1, source_target_pairs={{0,4},{4,0},{1,5},{5,1},{2,6},{6,2},{3,7},{7,3},{8,12},{12,8},{9,1... | collective-permute-start | bytes 663560 | tf_op jit(solution)/shard_map/ppermute | solution.py:1020
  42.8 5.1 %collective-permute-start.6 = (bf16[128,256]{1,0:T(8,128)(2,1)S(1)}, bf16[128,256]{1,0:T(8,128)(2,1)}, u32[]{:S(2)}, u32[]{:S(2)}) collective-permute-start(bf16[128,256]{1,0:T(8,128)(2,1)S(1)} %copy-done.88), channel_id=1, source_target_pairs={{0,2},{1,3},{2,0},{3,1},{4,6},{5,7},{6,4},{7,5},{8,10},{9,11},{10,... | collective-permute-start | bytes 196616 | tf_op jit(solution)/shard_map/ppermute | solution.py:1020
  51.9 3.3 collective-permute-done.10
  60.9 5.6 %collective-permute-done.11 = bf16[2,2,144,384]{3,2,1,0:T(8,128)(2,1)S(1)} collective-permute-done((bf16[2,2,144,384]{3,2,1,0:T(8,128)(2,1)S(1)}, bf16[2,2,144,384]{3,2,1,0:T(8,128)(2,1)S(1)}, u32[]{:S(2)}, u32[]{:S(2)}) %collective-permute-start.11) | collective-permute-done | bytes 442400 | tf_op jit(solution)/shard_map/ppermute | solution.py:1020
  73.9 6.2 %project.2 = (bf16[2048,256]{1,0:T(8,128)(2,1)S(1)}, bf16[2048,256]{1,0:T(8,128)(2,1)S(1)}, bf16[2048,256]{1,0:T(8,128)(2,1)S(1)}, bf16[8,256,1024]{2,1,0:T(8,128)(2,1)S(1)}) custom-call(s32[4]{0:T(128)S(1)} %gather_fusion.1, s32[4]{0:T(128)S(1)} %copy-done.65, bf16[2,256,1024]{2,1,0:T(8,128)(2,1)} %bitcast_select_fusion.near.x_ref, ...), custom_call_target="tpu_custom_call" | custom-call | flops 70000000 | bytes 1024 | tf_op jit(solution)/shard_map/project/pallas_call | solution.py:660
  80.2 9.5 %collective-permute-done.7 = bf16[256,512]{1,0:T(8,128)(2,1)S(1)} collective-permute-done((bf16[256,512]{1,0:T(8,128)(2,1)S(1)}, bf16[256,512]{1,0:T(8,128)(2,1)S(1)}, u32[]{:S(2)}, u32[]{:S(2)}) %collective-permute-start.7) | collective-permute-done | bytes 262176 | tf_op jit(solution)/shard_map/ppermute | solution.py:1020
  95.9 5.7 %project.3 = (bf16[2048,256]{1,0:T(8,128)(2,1)S(1)}, bf16[2048,256]{1,0:T(8,128)(2,1)S(1)}, bf16[2048,256]{1,0:T(8,128)(2,1)S(1)}, bf16[8,256,1024]{2,1,0:T(8,128)(2,1)S(1)}) custom-call(s32[4]{0:T(128)S(1)} %gather_fusion, s32[4]{0:T(128)S(1)} %copy-done.66, ...), custom_call_target="tpu_custom_call", output_to_operand_aliasing={{0}: (8, {}), {1}: (9, {}), {2}: (10, {}), {3}: (11, {})} | custom-call | flops 70000000 | bytes 1024 | tf_op jit(solution)/shard_map/project/pallas_call | solution.py:660
  103.6 7.2 %collective-permute-done.17 = bf16[256,512]{1,0:T(8,128)(2,1)S(1)} collective-permute-done((bf16[256,512]{1,0:T(8,128)(2,1)}, bf16[256,512]{1,0:T(8,128)(2,1)S(1)}, u32[]{:S(2)}, u32[]{:S(2)}) %collective-permute-start.17) | collective-permute-done | bytes 262176 | tf_op jit(solution)/shard_map/ppermute | solution.py:1020
  120.2 10.2 %attend.2 = (f32[2048,128]{1,0:T(8,128)S(1)}, bf16[8,256,128]{2,1,0:T(8,128)(2,1)S(1)}, f32[1,2,2048]{2,1,0:T(2,128)S(1)}) custom-call(s32[4,4]{1,0:T(4,128)S(1)} %pad_add_fusion.bounds, s32[8]{0:T(128)S(1)} %convert_add_fusion.6.slot_of, bf16[2048,256]{1,0:T(8,128)(2,1)S(1)} %copy-done.7, bf16[2048,256]{1,0:T(8,128)(2,1)S(1)} %copy-done.11, ...), custom_call_target="tpu_custom_call" | custom-call | flops 140000000 | bytes 1024 | tf_op jit(solution)/shard_map/attend/pallas_call | solution.py:427
  130.5 5.9 %collective-permute-done.20 = bf16[2,128,1024]{2,1,0:T(8,128)(2,1)S(1)} collective-permute-done((bf16[2,128,1024]{2,1,0:T(8,128)(2,1)S(1)}, bf16[2,128,1024]{2,1,0:T(8,128)(2,1)S(1)}, u32[]{:S(2)}, u32[]{:S(2)}) %collective-permute-start.20) | collective-permute-done | bytes 524320 | tf_op jit(solution)/shard_map/ppermute | solution.py:1020
  138.9 11.3 %attend.3 = (f32[2,2,2048]{2,1,0:T(2,128)S(1)}, bf16[8,256,128]{2,1,0:T(8,128)(2,1)S(1)}, f32[2048,128]{1,0:T(8,128)}) fusion(f32[2,2,2048]{2,1,0:T(2,128)S(1)} %constant_dynamic-update-slice_fusion.21, s32[4,4]{1,0:T(4,128)S(1)} %pad_add_fusion.bounds, s32[8]{0:T(128)S(1)} %convert_add_fusion.6.slot_of, bf16[2048,256]{1,0:T(8,128)(2,1)S(1)} %copy-done.7, ...), kind=kCustom, calls=%fused_computation.240 | custom fusion | flops 140000000 | bytes 5802496 | tf_op jit(solution)/shard_map/attend/pallas_call | solution.py:427
  156.7 2.9 collective-permute-done.24.far
  159.6 4.7 collective-permute-done.25.both
  164.4 3.7 mix.1
  171.5 4.7 collective-permute-start.28
  181.5 11.8 %add_convert_fusion = (bf16[1024,2048]{1,0:T(8,128)(2,1)}, bf16[1024,2048]{1,0:T(8,128)(2,1)S(1)}) fusion(bf16[1024,1024]{1,0:T(8,128)(2,1)} %constant_dynamic-update-slice_fusion.14, bf16[1024,2048]{1,0:T(8,128)(2,1)} %all-gather.2.cloned.1.call-done), kind=kOutput, calls=%fused_computation.3 | convolution fusion | flops 4330618880 | bytes 14680064 | tf_op jit(solution)/shard_map/dot_general | solution.py:1068
  193.3 6.6 %collective-permute-done.28 = bf16[2,128,2048]{2,1,0:T(8,128)(2,1)} collective-permute-done((bf16[2,128,2048]{2,1,0:T(8,128)(2,1)}, bf16[2,128,2048]{2,1,0:T(8,128)(2,1)}, u32[]{:S(2)}, u32[]{:S(2)}) %collective-permute-start.28) | collective-permute-done | bytes 1048608 | tf_op jit(solution)/shard_map/ppermute | solution.py:1020
  205.6 2.4 fusion.13
  209.5 2.4 fusion.7.terms_ref
  211.9 2.8 finish.1
  219.4 5.1 %convolution_convert_fusion.1.refs_1_.refs_3_.refs_5_.refs_7_ = bf16[1024,2048]{1,0:T(8,128)(2,1)S(1)} fusion(bf16[1024,1024]{1,0:T(8,128)(2,1)S(1)} %constant_dynamic-update-slice_fusion.16, bf16[1024,2048]{1,0:T(8,128)(2,1)S(1)} %copy-done.96), kind=kOutput, calls=%fused_computation.10 | convolution fusion | flops 4297064448 | bytes 10485760 | tf_op jit(solution)/shard_map/dot_general | solution.py:1068
  224.5 6.6 %multiply_convert_fusion = bf16[1024,2048]{1,0:T(8,128)(2,1)S(1)} fusion(bf16[1024,2048]{1,0:T(8,128)(2,1)} %get-tuple-element.197, bf16[1024,1024]{1,0:T(8,128)(2,1)S(1)} %constant_dynamic-update-slice_fusion.16, bf16[1024,2048]{1,0:T(8,128)(2,1)S(1)} %bitcast.300), kind=kOutput, calls=%fused_computation.2 | convolution fusion | flops 4301258752 | bytes 14680064 | tf_op jit(solution)/shard_map/dot_general | solution.py:1068
  231.1 2.4 fusion.16
  233.9 6.4 %convolution_convert_fusion.refs_0_.refs_2_.refs_4_.refs_6_ = bf16[1024,2048]{1,0:T(8,128)(2,1)S(1)} fusion(bf16[1024,1024]{1,0:T(8,128)(2,1)} %constant_dynamic-update-slice_fusion.14, bf16[1024,2048]{1,0:T(8,128)(2,1)S(1)} %multiply_convert_fusion), kind=kOutput, calls=%fused_computation.9 | convolution fusion | flops 4297064448 | bytes 10485760 | tf_op jit(solution)/shard_map/dot_general | solution.py:1068
  240.4 2.7 cut_lines.1
  250.8 4.4 turn.1
  260.1 3.9 collective-permute-done.36
  264.0 5.1 %collective-permute-done.34 = bf16[2,256,256]{2,1,0:T(8,128)(2,1)S(1)} collective-permute-done((bf16[2,256,256]{2,1,0:T(8,128)(2,1)S(1)}, bf16[2,256,256]{2,1,0:T(8,128)(2,1)S(1)}, u32[]{:S(2)}, u32[]{:S(2)}) %collective-permute-start.34) | collective-permute-done | bytes 262176 | tf_op jit(solution)/shard_map/ppermute | solution.py:1020
  279.7 19.0 %attend_back.2 = (bf16[4,256,768]{2,1,0:T(8,128)(2,1)S(1)}, f32[2,128,1024]{2,1,0:T(8,128)S(1)}) custom-call(s32[4,4]{1,0:T(4,128)S(1)} %pad_add_fusion.bounds, s32[8]{0:T(128)S(1)} %convert_add_fusion.6.slot_of, bf16[2048,256]{1,0:T(8,128)(2,1)S(1)} %copy-done.8, bf16[2048,256]{1,0:T(8,128)(2,1)S(1)} %copy-done.12, bf16[2048,256]{1,0:T(8,128)(2,1)S(1)} %copy-done.16, ...), custom_call_target="tpu_custom_call" | custom-call | flops 230000000 | bytes 1024 | tf_op jit(solution)/shard_map/attend_back/pallas_call | solution.py:573
  306.4 2.5 add_convert_fusion.6
  309.3 2.6 fusion.20
  311.9 11.0 %collective-permute-start.44 = (bf16[224,2048]{1,0:T(8,128)(2,1)}, bf16[224,2048]{1,0:T(8,128)(2,1)}, u32[]{:S(2)}, u32[]{:S(2)}) collective-permute-start(bf16[224,2048]{1,0:T(8,128)(2,1)} %fusion.20), channel_id=1, source_target_pairs={{0,16},{8,24},{16,0},{24,8},{1,17},{9,25},{17,1},{25,9},{2,18},{10... | collective-permute-start | bytes 2752520 | tf_op jit(solution)/shard_map/ppermute | solution.py:1020
  322.9 2.5 fusion.21
  330.4 3.6 fusion.90
  336.0 14.6 %attend_back.3 = bf16[4,256,768]{2,1,0:T(8,128)(2,1)S(1)} custom-call(s32[4,4]{1,0:T(4,128)S(1)} %pad_add_fusion.bounds, s32[8]{0:T(128)S(1)} %convert_add_fusion.6.slot_of, bf16[2048,256]{1,0:T(8,128)(2,1)S(1)} %copy-done.9, bf16[2048,256]{1,0:T(8,128)(2,1)S(1)} %copy-done.13, bf16[2048,256]{1,0:T(8,128)(2,1)S(1)} %copy-done.17, ...), custom_call_target="tpu_custom_call" | custom-call | flops 230000000 | bytes 1024 | tf_op jit(solution)/shard_map/attend_back/pallas_call | solution.py:573
  354.0 3.4 multiply_reduce_fusion
  361.6 2.6 add_convert_fusion.5
  364.1 2.8 convert_add_fusion.2.keep_ref
  366.9 3.4 spread_first.1
  374.4 15.4 %collective-permute-done.49.low_far = bf16[2,11,128,128]{3,2,1,0:T(8,128)(2,1)} collective-permute-done((bf16[2,11,128,128]{3,2,1,0:T(8,128)(2,1)}, bf16[2,11,128,128]{3,2,1,0:T(8,128)(2,1)}, u32[]{:S(2)}, u32[]{:S(2)}) %collective-permute-start.49) | collective-permute-done | bytes 720928 | tf_op jit(solution)/shard_map/ppermute | solution.py:1020
  392.7 3.0 spread_second.1
  406.8 11.1 %collective-permute-done.51.low_far = bf16[11,128,128]{2,1,0:T(8,128)(2,1)S(1)} collective-permute-done((bf16[11,128,128]{2,1,0:T(8,128)(2,1)}, bf16[11,128,128]{2,1,0:T(8,128)(2,1)S(1)}, u32[]{:S(2)}, u32[]{:S(2)}) %collective-permute-start.51) | collective-permute-done | bytes 360480 | tf_op jit(solution)/shard_map/ppermute | solution.py:1020
  418.7 11.9 %collective-permute-start.56 = (bf16[11,128,128]{2,1,0:T(8,128)(2,1)S(1)}, bf16[11,128,128]{2,1,0:T(8,128)(2,1)S(1)}, u32[]{:S(2)}, u32[]{:S(2)}) collective-permute-start(bf16[11,128,128]{2,1,0:T(8,128)(2,1)S(1)} %get-tuple-element.256), channel_id=1, source_target_pairs={{0,2},{1,3},{2,0},{3,1},{4,6},{5,7},{6,4},{7,5},{8,10},{9,11},{10,... | collective-permute-start | bytes 1081352 | tf_op jit(solution)/shard_map/ppermute | solution.py:1020
  434.1 21.7 %collective-permute-done.56.far = bf16[11,128,128]{2,1,0:T(8,128)(2,1)S(1)} collective-permute-done((bf16[11,128,128]{2,1,0:T(8,128)(2,1)S(1)}, bf16[11,128,128]{2,1,0:T(8,128)(2,1)S(1)}, u32[]{:S(2)}, u32[]{:S(2)}) %collective-permute-start.56) | collective-permute-done | bytes 360480 | tf_op jit(solution)/shard_map/ppermute | solution.py:1020
  456.5 9.1 %collective-permute-done.59 = bf16[448,512]{1,0:T(8,128)(2,1)S(1)} collective-permute-done((bf16[448,512]{1,0:T(8,128)(2,1)S(1)}, bf16[448,512]{1,0:T(8,128)(2,1)S(1)}, u32[]{:S(2)}, u32[]{:S(2)}) %collective-permute-start.59) | collective-permute-done | bytes 458784 | tf_op jit(solution)/shard_map/ppermute | solution.py:1020
  (470 shorter events, 154.3 us)
Async XLA Ops:
  7.2 174.3 %all-gather.2.cloned.1.call-start = ((), (), s32[]{:S(2)}) async-start(), calls=%async_computation | async-start | bytes 5242880 | tf_op jit(solution)/shard_map/all_gather | solution.py:1250
  8.3 14.3 %collective-permute-start = (bf16[144,768]{1,0:T(8,128)(2,1)S(1)}, bf16[144,768]{1,0:T(8,128)(2,1)S(1)}, u32[]{:S(2)}, u32[]{:S(2)}) collective-permute-start(bf16[144,768]{1,0:T(8,128)(2,1)S(1)} %fusion.57), channel_id=1, source_target_pairs={{0,2},{1,3},{2,0},{3,1},{4,6},{5,7},{6,4},{7,5},{8,10},{9,11},{10,... | collective-permute-start | bytes 663560 | tf_op jit(solution)/shard_map/ppermute | solution.py:1020
  22.8 35.8 %collective-permute-start.2 = (bf16[2,256,1024]{2,1,0:T(8,128)(2,1)}, bf16[2,256,1024]{2,1,0:T(8,128)(2,1)}, u32[]{:S(2)}, u32[]{:S(2)}) collective-permute-start(bf16[2,256,1024]{2,1,0:T(8,128)(2,1)} %bitcast.6), channel_id=1, source_target_pairs={{4,2},{2,4},{5,3},{3,5},{12,10},{10,12},{13,11},{11,13},{20,18},{1... | collective-permute-start | bytes 3145736 | tf_op jit(solution)/shard_map/ppermute | solution.py:1030
  35.6 12.3 %collective-permute-start.9 = (bf16[144,768]{1,0:T(8,128)(2,1)S(1)}, bf16[144,768]{1,0:T(8,128)(2,1)S(1)}, u32[]{:S(2)}, u32[]{:S(2)}) collective-permute-start(bf16[144,768]{1,0:T(8,128)(2,1)S(1)} %pad_maximum_fusion.21), channel_id=1, source_target_pairs={{0,4},{4,0},{1,5},{5,1},{2,6},{6,2},{3,7},{7,3},{8,12},{12,8},{9,1... | collective-permute-start | bytes 663560 | tf_op jit(solution)/shard_map/ppermute | solution.py:1020
  42.8 25.9 %collective-permute-start.6 = (bf16[128,256]{1,0:T(8,128)(2,1)S(1)}, bf16[128,256]{1,0:T(8,128)(2,1)}, u32[]{:S(2)}, u32[]{:S(2)}) collective-permute-start(bf16[128,256]{1,0:T(8,128)(2,1)S(1)} %copy-done.88), channel_id=1, source_target_pairs={{0,2},{1,3},{2,0},{3,1},{4,6},{5,7},{6,4},{7,5},{8,10},{9,11},{10,... | collective-permute-start | bytes 196616 | tf_op jit(solution)/shard_map/ppermute | solution.py:1020
  55.3 11.2 %collective-permute-start.11 = (bf16[2,2,144,384]{3,2,1,0:T(8,128)(2,1)S(1)}, bf16[2,2,144,384]{3,2,1,0:T(8,128)(2,1)S(1)}, u32[]{:S(2)}, u32[]{:S(2)}) collective-permute-start(bf16[2,2,144,384]{3,2,1,0:T(8,128)(2,1)S(1)} %pad_maximum_fusion.19), channel_id=1, source_target_pairs={{0,16},{8,24},{16,0},{24,8},{1,17},{9,25},{17,1},{25,9},{2,18},{10... | collective-permute-start | bytes 1327112 | tf_op jit(solution)/shard_map/ppermute | solution.py:1020
  57.0 10.8 %collective-permute-start.13 = (bf16[2,2,144,384]{3,2,1,0:T(8,128)(2,1)S(1)}, bf16[2,2,144,384]{3,2,1,0:T(8,128)(2,1)S(1)}, u32[]{:S(2)}, u32[]{:S(2)}) collective-permute-start(bf16[2,2,144,384]{3,2,1,0:T(8,128)(2,1)S(1)} %pad_maximum_fusion.20), channel_id=1, source_target_pairs={{0,8},{8,0},{16,24},{24,16},{1,9},{9,1},{17,25},{25,17},{2,10},{10... | collective-permute-start | bytes 1327112 | tf_op jit(solution)/shard_map/ppermute | solution.py:1020
  60.9 31.1 %collective-permute-start.3 = (bf16[2,256,1024]{2,1,0:T(8,128)(2,1)}, bf16[2,256,1024]{2,1,0:T(8,128)(2,1)}, u32[]{:S(2)}, u32[]{:S(2)}) collective-permute-start(bf16[2,256,1024]{2,1,0:T(8,128)(2,1)} %bitcast_select_fusion.near.x_ref), channel_id=1, source_target_pairs={{0,1},{1,0},{2,3},{3,2},{4,5},{5,4},{6,7},{7,6},{8,9},{9,8},{10,11... | collective-permute-start | bytes 3145736 | tf_op jit(solution)/shard_map/ppermute | solution.py:1020
  60.9 11.6 %collective-permute-start.8 = (bf16[2,256,1024]{2,1,0:T(8,128)(2,1)}, bf16[2,256,1024]{2,1,0:T(8,128)(2,1)}, u32[]{:S(2)}, u32[]{:S(2)}) collective-permute-start(bf16[2,256,1024]{2,1,0:T(8,128)(2,1)} %bitcast_select_fusion.near.x_ref), channel_id=1, source_target_pairs={{0,4},{4,0},{1,5},{5,1},{2,6},{6,2},{3,7},{7,3},{8,12},{12,8},{9,1... | collective-permute-start | bytes 3145736 | tf_op jit(solution)/shard_map/ppermute | solution.py:1020
  68.7 20.9 %collective-permute-start.7 = (bf16[256,512]{1,0:T(8,128)(2,1)S(1)}, bf16[256,512]{1,0:T(8,128)(2,1)S(1)}, u32[]{:S(2)}, u32[]{:S(2)}) collective-permute-start(bf16[256,512]{1,0:T(8,128)(2,1)S(1)} %get-tuple-element.160), channel_id=1, source_target_pairs={{0,2},{1,3},{2,0},{3,1},{4,6},{5,7},{6,4},{7,5},{8,10},{9,11},{10,... | collective-permute-start | bytes 786440 | tf_op jit(solution)/shard_map/ppermute | solution.py:1020
  71.2 22.1 %collective-permute-start.15 = (bf16[128,512]{1,0:T(8,128)(2,1)S(1)}, bf16[128,512]{1,0:T(8,128)(2,1)S(1)}, u32[]{:S(2)}, u32[]{:S(2)}) collective-permute-start(bf16[128,512]{1,0:T(8,128)(2,1)S(1)} %pad_maximum_fusion.28), channel_id=1, source_target_pairs={{0,1},{1,0},{2,3},{3,2},{4,5},{5,4},{6,7},{7,6},{8,9},{9,8},{10,11... | collective-permute-start | bytes 393224 | tf_op jit(solution)/shard_map/ppermute | solution.py:1020
  93.4 18.7 %collective-permute-start.16 = (bf16[256,1024]{1,0:T(8,128)(2,1)S(1)}, bf16[256,1024]{1,0:T(8,128)(2,1)S(1)}, u32[]{:S(2)}, u32[]{:S(2)}) collective-permute-start(bf16[256,1024]{1,0:T(8,128)(2,1)S(1)} %pad_maximum_fusion.13), channel_id=1, source_target_pairs={{0,1},{1,0},{2,3},{3,2},{4,5},{5,4},{6,7},{7,6},{8,9},{9,8},{10,11... | collective-permute-start | bytes 1572872 | tf_op jit(solution)/shard_map/ppermute | solution.py:1020
  93.7 17.1 %collective-permute-start.17 = (bf16[256,512]{1,0:T(8,128)(2,1)}, bf16[256,512]{1,0:T(8,128)(2,1)S(1)}, u32[]{:S(2)}, u32[]{:S(2)}) collective-permute-start(bf16[256,512]{1,0:T(8,128)(2,1)} %get-tuple-element.169), channel_id=1, source_target_pairs={{0,2},{1,3},{2,0},{3,1},{4,6},{5,7},{6,4},{7,5},{8,10},{9,11},{10,... | collective-permute-start | bytes 786440 | tf_op jit(solution)/shard_map/ppermute | solution.py:1020
  95.0 15.8 %collective-permute-start.18 = (bf16[1,128,1024]{2,1,0:T(8,128)(2,1)S(1)}, bf16[1,128,1024]{2,1,0:T(8,128)(2,1)S(1)}, u32[]{:S(2)}, u32[]{:S(2)}) collective-permute-start(bf16[1,128,1024]{2,1,0:T(8,128)(2,1)S(1)} %maximum_bitcast_fusion.2), channel_id=1, source_target_pairs={{0,8},{8,0},{16,24},{24,16},{1,9},{9,1},{17,25},{25,17},{2,10},{10... | collective-permute-start | bytes 786440 | tf_op jit(solution)/shard_map/ppermute | solution.py:1020
  114.2 16.3 %collective-permute-start.19 = (bf16[256,1024]{1,0:T(8,128)(2,1)}, bf16[256,1024]{1,0:T(8,128)(2,1)}, u32[]{:S(2)}, u32[]{:S(2)}) collective-permute-start(bf16[256,1024]{1,0:T(8,128)(2,1)} %pad_maximum_fusion.15), channel_id=1, source_target_pairs={{0,1},{1,0},{2,3},{3,2},{4,5},{5,4},{6,7},{7,6},{8,9},{9,8},{10,11... | collective-permute-start | bytes 1572872 | tf_op jit(solution)/shard_map/ppermute | solution.py:1020
  118.1 18.3 %collective-permute-start.20 = (bf16[2,128,1024]{2,1,0:T(8,128)(2,1)S(1)}, bf16[2,128,1024]{2,1,0:T(8,128)(2,1)S(1)}, u32[]{:S(2)}, u32[]{:S(2)}) collective-permute-start(bf16[2,128,1024]{2,1,0:T(8,128)(2,1)S(1)} %pad_maximum_fusion.14), channel_id=1, source_target_pairs={{0,16},{8,24},{16,0},{24,8},{1,17},{9,25},{17,1},{25,9},{2,18},{10... | collective-permute-start | bytes 1572872 | tf_op jit(solution)/shard_map/ppermute | solution.py:1020
  138.0 14.3 %collective-permute-start.21 = (bf16[1,128,2048]{2,1,0:T(8,128)(2,1)S(1)}, bf16[1,128,2048]{2,1,0:T(8,128)(2,1)S(1)}, u32[]{:S(2)}, u32[]{:S(2)}) collective-permute-start(bf16[1,128,2048]{2,1,0:T(8,128)(2,1)S(1)} %get-tuple-element.182), channel_id=1, source_target_pairs={{0,8},{8,0},{16,24},{24,16},{1,9},{9,1},{17,25},{25,17},{2,10},{10... | collective-permute-start | bytes 1572872 | tf_op jit(solution)/shard_map/ppermute | solution.py:1020
  138.1 15.4 %collective-permute-start.22 = (bf16[1,128,2048]{2,1,0:T(8,128)(2,1)S(1)}, bf16[1,128,2048]{2,1,0:T(8,128)(2,1)S(1)}, u32[]{:S(2)}, u32[]{:S(2)}) collective-permute-start(bf16[1,128,2048]{2,1,0:T(8,128)(2,1)S(1)} %get-tuple-element.184), channel_id=1, source_target_pairs={{0,16},{8,24},{16,0},{24,8},{1,17},{9,25},{17,1},{25,9},{2,18},{10... | collective-permute-start | bytes 1572872 | tf_op jit(solution)/shard_map/ppermute | solution.py:1020
  150.5 9.2 %collective-permute-start.24 = (bf16[2,256,256]{2,1,0:T(8,128)(2,1)S(1)}, bf16[2,256,256]{2,1,0:T(8,128)(2,1)S(1)}, u32[]{:S(2)}, u32[]{:S(2)}) collective-permute-start(bf16[2,256,256]{2,1,0:T(8,128)(2,1)S(1)} %get-tuple-element.341), channel_id=1, source_target_pairs={{0,1},{1,0},{2,3},{3,2},{4,5},{5,4},{6,7},{7,6},{8,9},{9,8},{10,11... | collective-permute-start | bytes 786440 | tf_op jit(solution)/shard_map/ppermute | solution.py:1020
  150.5 13.8 %collective-permute-start.25 = (bf16[2,256,256]{2,1,0:T(8,128)(2,1)S(1)}, bf16[2,256,256]{2,1,0:T(8,128)(2,1)S(1)}, u32[]{:S(2)}, u32[]{:S(2)}) collective-permute-start(bf16[2,256,256]{2,1,0:T(8,128)(2,1)S(1)} %get-tuple-element.340), channel_id=1, source_target_pairs={{0,5},{1,4},{2,7},{3,6},{4,1},{5,0},{6,3},{7,2},{8,13},{9,12},{10,... | collective-permute-start | bytes 786440 | tf_op jit(solution)/shard_map/ppermute | solution.py:1062
  170.8 9.7 %collective-permute-start.27 = (bf16[512,1024]{1,0:T(8,128)(2,1)S(1)}, bf16[512,1024]{1,0:T(8,128)(2,1)S(1)}, u32[]{:S(2)}, u32[]{:S(2)}) collective-permute-start(bf16[512,1024]{1,0:T(8,128)(2,1)S(1)} %get-tuple-element.189), channel_id=1, source_target_pairs={{0,4},{4,0},{1,5},{5,1},{2,6},{6,2},{3,7},{7,3},{8,12},{12,8},{9,1... | collective-permute-start | bytes 3145736 | tf_op jit(solution)/shard_map/ppermute | solution.py:1020
  171.5 28.4 %collective-permute-start.28 = (bf16[2,128,2048]{2,1,0:T(8,128)(2,1)}, bf16[2,128,2048]{2,1,0:T(8,128)(2,1)}, u32[]{:S(2)}, u32[]{:S(2)}) collective-permute-start(bf16[2,128,2048]{2,1,0:T(8,128)(2,1)} %pad_maximum_fusion.8), channel_id=1, source_target_pairs={{0,16},{8,24},{16,0},{24,8},{1,17},{9,25},{17,1},{25,9},{2,18},{10... | collective-permute-start | bytes 3145736 | tf_op jit(solution)/shard_map/ppermute | solution.py:1020
  176.2 25.1 %collective-permute-start.29 = (bf16[2,1,128,2048]{3,2,1,0:T(8,128)(2,1)}, bf16[2,1,128,2048]{3,2,1,0:T(8,128)(2,1)}, u32[]{:S(2)}, u32[]{:S(2)}) collective-permute-start(bf16[2,1,128,2048]{3,2,1,0:T(8,128)(2,1)} %maximum_bitcast_fusion.1), channel_id=1, source_target_pairs={{0,8},{8,0},{16,24},{24,16},{1,9},{9,1},{17,25},{25,17},{2,10},{10... | collective-permute-start | bytes 3145736 | tf_op jit(solution)/shard_map/ppermute | solution.py:1020
  177.8 30.3 %collective-permute-start.31 = (bf16[512,1024]{1,0:T(8,128)(2,1)}, bf16[512,1024]{1,0:T(8,128)(2,1)}, u32[]{:S(2)}, u32[]{:S(2)}) collective-permute-start(bf16[512,1024]{1,0:T(8,128)(2,1)} %bitcast.40), channel_id=1, source_target_pairs={{4,2},{2,4},{5,3},{3,5},{12,10},{10,12},{13,11},{11,13},{20,18},{1... | collective-permute-start | bytes 3145736 | tf_op jit(solution)/shard_map/ppermute | solution.py:1030
  233.5 16.5 %collective-permute-start.33 = (bf16[512,1024]{1,0:T(8,128)(2,1)S(1)}, bf16[512,1024]{1,0:T(8,128)(2,1)S(1)}, u32[]{:S(2)}, u32[]{:S(2)}) collective-permute-start(bf16[512,1024]{1,0:T(8,128)(2,1)S(1)} %fusion.16), channel_id=1, source_target_pairs={{0,4},{4,0},{1,5},{5,1},{2,6},{6,2},{3,7},{7,3},{8,12},{12,8},{9,1... | collective-permute-start | bytes 3145736 | tf_op jit(solution)/shard_map/ppermute | solution.py:1020
  245.6 53.1 %collective-permute-start.39 = (bf16[2,224,2048]{2,1,0:T(8,128)(2,1)}, bf16[2,224,2048]{2,1,0:T(8,128)(2,1)}, u32[]{:S(2)}, u32[]{:S(2)}) collective-permute-start(bf16[2,224,2048]{2,1,0:T(8,128)(2,1)} %get-tuple-element.198), channel_id=1, source_target_pairs={{0,8},{8,0},{16,24},{24,16},{1,9},{9,1},{17,25},{25,17},{2,10},{10... | collective-permute-start | bytes 5505032 | tf_op jit(solution)/shard_map/ppermute | solution.py:1020
  247.2 51.6 %collective-permute-start.40 = (bf16[2,224,2048]{2,1,0:T(8,128)(2,1)}, bf16[2,224,2048]{2,1,0:T(8,128)(2,1)}, u32[]{:S(2)}, u32[]{:S(2)}) collective-permute-start(bf16[2,224,2048]{2,1,0:T(8,128)(2,1)} %get-tuple-element.199), channel_id=1, source_target_pairs={{0,16},{8,24},{16,0},{24,8},{1,17},{9,25},{17,1},{25,9},{2,18},{10... | collective-permute-start | bytes 5505032 | tf_op jit(solution)/shard_map/ppermute | solution.py:1020
  255.3 8.7 %collective-permute-start.36 = (bf16[2,256,256]{2,1,0:T(8,128)(2,1)S(1)}, bf16[2,256,256]{2,1,0:T(8,128)(2,1)S(1)}, u32[]{:S(2)}, u32[]{:S(2)}) collective-permute-start(bf16[2,256,256]{2,1,0:T(8,128)(2,1)S(1)} %get-tuple-element.337), channel_id=1, source_target_pairs={{0,5},{1,4},{2,7},{3,6},{4,1},{5,0},{6,3},{7,2},{8,13},{9,12},{10,... | collective-permute-start | bytes 786440 | tf_op jit(solution)/shard_map/ppermute | solution.py:1062
  255.4 8.6 %collective-permute-start.35 = (bf16[2,256,256]{2,1,0:T(8,128)(2,1)S(1)}, bf16[2,256,256]{2,1,0:T(8,128)(2,1)S(1)}, u32[]{:S(2)}, u32[]{:S(2)}) collective-permute-start(bf16[2,256,256]{2,1,0:T(8,128)(2,1)S(1)} %get-tuple-element.338), channel_id=1, source_target_pairs={{0,4},{4,0},{1,5},{5,1},{2,6},{6,2},{3,7},{7,3},{8,12},{12,8},{9,1... | collective-permute-start | bytes 786440 | tf_op jit(solution)/shard_map/ppermute | solution.py:1020
  255.8 13.3 %collective-permute-start.34 = (bf16[2,256,256]{2,1,0:T(8,128)(2,1)S(1)}, bf16[2,256,256]{2,1,0:T(8,128)(2,1)S(1)}, u32[]{:S(2)}, u32[]{:S(2)}) collective-permute-start(bf16[2,256,256]{2,1,0:T(8,128)(2,1)S(1)} %get-tuple-element.339), channel_id=1, source_target_pairs={{0,1},{1,0},{2,3},{3,2},{4,5},{5,4},{6,7},{7,6},{8,9},{9,8},{10,11... | collective-permute-start | bytes 786440 | tf_op jit(solution)/shard_map/ppermute | solution.py:1020
  270.2 28.6 %collective-permute-start.37 = (bf16[512,1024]{1,0:T(8,128)(2,1)}, bf16[512,1024]{1,0:T(8,128)(2,1)}, u32[]{:S(2)}, u32[]{:S(2)}) collective-permute-start(bf16[512,1024]{1,0:T(8,128)(2,1)} %get-tuple-element.257), channel_id=1, source_target_pairs={{4,2},{2,4},{5,3},{3,5},{12,10},{10,12},{13,11},{11,13},{20,18},{1... | collective-permute-start | bytes 3145736 | tf_op jit(solution)/shard_map/ppermute | solution.py:1030
  272.8 25.9 %collective-permute-start.38 = (bf16[2,256,512]{2,1,0:T(8,128)(2,1)}, bf16[2,256,512]{2,1,0:T(8,128)(2,1)}, u32[]{:S(2)}, u32[]{:S(2)}) collective-permute-start(bf16[2,256,512]{2,1,0:T(8,128)(2,1)} %get-tuple-element.331), channel_id=1, source_target_pairs={{0,1},{1,0},{2,3},{3,2},{4,5},{5,4},{6,7},{7,6},{8,9},{9,8},{10,11... | collective-permute-start | bytes 1572872 | tf_op jit(solution)/shard_map/ppermute | solution.py:1020
  309.0 41.7 %collective-permute-start.43 = (bf16[4,128,1024]{2,1,0:T(8,128)(2,1)}, bf16[4,128,1024]{2,1,0:T(8,128)(2,1)S(1)}, u32[]{:S(2)}, u32[]{:S(2)}) collective-permute-start(bf16[4,128,1024]{2,1,0:T(8,128)(2,1)} %dynamic-slice_bitcast_fusion), channel_id=1, source_target_pairs={{0,4},{4,0},{1,5},{5,1},{2,6},{6,2},{3,7},{7,3},{8,12},{12,8},{9,1... | collective-permute-start | bytes 3145736 | tf_op jit(solution)/shard_map/ppermute | solution.py:1020
  311.9 38.7 %collective-permute-start.44 = (bf16[224,2048]{1,0:T(8,128)(2,1)}, bf16[224,2048]{1,0:T(8,128)(2,1)}, u32[]{:S(2)}, u32[]{:S(2)}) collective-permute-start(bf16[224,2048]{1,0:T(8,128)(2,1)} %fusion.20), channel_id=1, source_target_pairs={{0,16},{8,24},{16,0},{24,8},{1,17},{9,25},{17,1},{25,9},{2,18},{10... | collective-permute-start | bytes 2752520 | tf_op jit(solution)/shard_map/ppermute | solution.py:1020
  325.4 25.2 %collective-permute-start.45 = (bf16[224,2048]{1,0:T(8,128)(2,1)}, bf16[224,2048]{1,0:T(8,128)(2,1)}, u32[]{:S(2)}, u32[]{:S(2)}) collective-permute-start(bf16[224,2048]{1,0:T(8,128)(2,1)} %fusion.21), channel_id=1, source_target_pairs={{0,8},{8,0},{16,24},{24,16},{1,9},{9,1},{17,25},{25,17},{2,10},{10... | collective-permute-start | bytes 2752520 | tf_op jit(solution)/shard_map/ppermute | solution.py:1020
  327.6 23.0 %collective-permute-start.42 = (bf16[256,512]{1,0:T(8,128)(2,1)S(1)}, bf16[256,512]{1,0:T(8,128)(2,1)S(1)}, u32[]{:S(2)}, u32[]{:S(2)}) collective-permute-start(bf16[256,512]{1,0:T(8,128)(2,1)S(1)} %copy-done.86), channel_id=1, source_target_pairs={{0,2},{1,3},{2,0},{3,1},{4,6},{5,7},{6,4},{7,5},{8,10},{9,11},{10,... | collective-permute-start | bytes 786440 | tf_op jit(solution)/shard_map/ppermute | solution.py:1020
  328.6 22.1 %collective-permute-start.46 = (bf16[256,1024]{1,0:T(8,128)(2,1)}, bf16[256,1024]{1,0:T(8,128)(2,1)S(1)}, u32[]{:S(2)}, u32[]{:S(2)}) collective-permute-start(bf16[256,1024]{1,0:T(8,128)(2,1)} %add_convert_fusion.6), channel_id=1, source_target_pairs={{0,1},{1,0},{2,3},{3,2},{4,5},{5,4},{6,7},{7,6},{8,9},{9,8},{10,11... | collective-permute-start | bytes 1572872 | tf_op jit(solution)/shard_map/ppermute | solution.py:1020
  371.2 19.8 %collective-permute-start.50 = (bf16[2,12,128,128]{3,2,1,0:T(8,128)(2,1)}, bf16[2,12,128,128]{3,2,1,0:T(8,128)(2,1)}, u32[]{:S(2)}, u32[]{:S(2)}) collective-permute-start(bf16[2,12,128,128]{3,2,1,0:T(8,128)(2,1)} %get-tuple-element.248), channel_id=1, source_target_pairs={{0,16},{8,24},{16,0},{24,8},{1,17},{9,25},{17,1},{25,9},{2,18},{10... | collective-permute-start | bytes 2359304 | tf_op jit(solution)/shard_map/ppermute | solution.py:1020
  371.2 18.6 %collective-permute-start.49 = (bf16[2,11,128,128]{3,2,1,0:T(8,128)(2,1)}, bf16[2,11,128,128]{3,2,1,0:T(8,128)(2,1)}, u32[]{:S(2)}, u32[]{:S(2)}) collective-permute-start(bf16[2,11,128,128]{3,2,1,0:T(8,128)(2,1)} %get-tuple-element.246), channel_id=1, source_target_pairs={{0,8},{8,0},{16,24},{24,16},{1,9},{9,1},{17,25},{25,17},{2,10},{10... | collective-permute-start | bytes 2162696 | tf_op jit(solution)/shard_map/ppermute | solution.py:1020
  373.2 28.2 %collective-permute-start.54 = (bf16[256,1024]{1,0:T(8,128)(2,1)S(1)}, bf16[256,1024]{1,0:T(8,128)(2,1)S(1)}, u32[]{:S(2)}, u32[]{:S(2)}) collective-permute-start(bf16[256,1024]{1,0:T(8,128)(2,1)S(1)} %copy-done.39), channel_id=1, source_target_pairs={{4,2},{2,4},{5,3},{3,5},{12,10},{10,12},{13,11},{11,13},{20,18},{1... | collective-permute-start | bytes 1572872 | tf_op jit(solution)/shard_map/ppermute | solution.py:1030
  374.1 27.3 %collective-permute-start.53 = (bf16[256,1024]{1,0:T(8,128)(2,1)}, bf16[256,1024]{1,0:T(8,128)(2,1)S(1)}, u32[]{:S(2)}, u32[]{:S(2)}) collective-permute-start(bf16[256,1024]{1,0:T(8,128)(2,1)} %add_convert_fusion.5), channel_id=1, source_target_pairs={{0,1},{1,0},{2,3},{3,2},{4,5},{5,4},{6,7},{7,6},{8,9},{9,8},{10,11... | collective-permute-start | bytes 1572872 | tf_op jit(solution)/shard_map/ppermute | solution.py:1020
  401.1 29.4 %collective-permute-start.58 = (bf16[2,448,512]{2,1,0:T(8,128)(2,1)}, bf16[2,448,512]{2,1,0:T(8,128)(2,1)}, u32[]{:S(2)}, u32[]{:S(2)}) collective-permute-start(bf16[2,448,512]{2,1,0:T(8,128)(2,1)} %get-tuple-element.323), channel_id=1, source_target_pairs={{0,1},{1,0},{2,3},{3,2},{4,5},{5,4},{6,7},{7,6},{8,9},{9,8},{10,11... | collective-permute-start | bytes 2752520 | tf_op jit(solution)/shard_map/ppermute | solution.py:1020
  402.9 15.0 %collective-permute-start.55 = (bf16[256,1024]{1,0:T(8,128)(2,1)S(1)}, bf16[256,1024]{1,0:T(8,128)(2,1)}, u32[]{:S(2)}, u32[]{:S(2)}) collective-permute-start(bf16[256,1024]{1,0:T(8,128)(2,1)S(1)} %end.3), channel_id=1, source_target_pairs={{4,2},{2,4},{5,3},{3,5},{12,10},{10,12},{13,11},{11,13},{20,18},{1... | collective-permute-start | bytes 1572872 | tf_op jit(solution)/shard_map/ppermute | solution.py:1030
  404.3 13.5 %collective-permute-start.52 = (bf16[12,128,128]{2,1,0:T(8,128)(2,1)}, bf16[12,128,128]{2,1,0:T(8,128)(2,1)S(1)}, u32[]{:S(2)}, u32[]{:S(2)}) collective-permute-start(bf16[12,128,128]{2,1,0:T(8,128)(2,1)} %get-tuple-element.251), channel_id=1, source_target_pairs={{0,8},{8,0},{16,24},{24,16},{1,9},{9,1},{17,25},{25,17},{2,10},{10... | collective-permute-start | bytes 1179656 | tf_op jit(solution)/shard_map/ppermute | solution.py:1020
  406.4 11.5 %collective-permute-start.51 = (bf16[11,128,128]{2,1,0:T(8,128)(2,1)}, bf16[11,128,128]{2,1,0:T(8,128)(2,1)S(1)}, u32[]{:S(2)}, u32[]{:S(2)}) collective-permute-start(bf16[11,128,128]{2,1,0:T(8,128)(2,1)} %get-tuple-element.250), channel_id=1, source_target_pairs={{0,16},{8,24},{16,0},{24,8},{1,17},{9,25},{17,1},{25,9},{2,18},{10... | collective-permute-start | bytes 1081352 | tf_op jit(solution)/shard_map/ppermute | solution.py:1020
  418.7 37.1 %collective-permute-start.56 = (bf16[11,128,128]{2,1,0:T(8,128)(2,1)S(1)}, bf16[11,128,128]{2,1,0:T(8,128)(2,1)S(1)}, u32[]{:S(2)}, u32[]{:S(2)}) collective-permute-start(bf16[11,128,128]{2,1,0:T(8,128)(2,1)S(1)} %get-tuple-element.256), channel_id=1, source_target_pairs={{0,2},{1,3},{2,0},{3,1},{4,6},{5,7},{6,4},{7,5},{8,10},{9,11},{10,... | collective-permute-start | bytes 1081352 | tf_op jit(solution)/shard_map/ppermute | solution.py:1020
  431.7 33.9 %collective-permute-start.59 = (bf16[448,512]{1,0:T(8,128)(2,1)S(1)}, bf16[448,512]{1,0:T(8,128)(2,1)S(1)}, u32[]{:S(2)}, u32[]{:S(2)}) collective-permute-start(bf16[448,512]{1,0:T(8,128)(2,1)S(1)} %fusion.27), channel_id=1, source_target_pairs={{0,2},{1,3},{2,0},{3,1},{4,6},{5,7},{6,4},{7,5},{8,10},{9,11},{10,... | collective-permute-start | bytes 1376264 | tf_op jit(solution)/shard_map/ppermute | solution.py:1020
  456.4 12.6 %collective-permute-start.57 = (bf16[5,128,128]{2,1,0:T(8,128)(2,1)S(1)}, bf16[5,128,128]{2,1,0:T(8,128)(2,1)S(1)}, u32[]{:S(2)}, u32[]{:S(2)}) collective-permute-start(bf16[5,128,128]{2,1,0:T(8,128)(2,1)S(1)} %get-tuple-element.260), channel_id=1, source_target_pairs={{0,1},{1,0},{2,3},{3,2},{4,5},{5,4},{6,7},{7,6},{8,9},{9,8},{10,11... | collective-permute-start | bytes 491528 | tf_op jit(solution)/shard_map/ppermute | solution.py:1020
  (111 other events, 643.8 us)
Sparse Core Ops, SparseCore 0:
  117.0 58.1 all-gather.1
where the time goes:
time: 486 us; the launch traced here: 479 us
  waiting for transfers between devices  133 us (27%)
  starting transfers between devices  86.3 us (18%)
  Pallas kernels  80.2 us (17%)
  other arithmetic  63.3 us (13%)
  matrix products  61.4 us (13%)
  local copies, waits for them, and re-layouts  39.2 us (8%)
  between operations  16.2 us (3%)
    ppermute x54, waiting for transfers between devices, flip(): lax.ppermute(plain(x), axis, [(i, i ^ bit) for i in range(lax.axis_size(a...  124 us
    ppermute x54, starting transfers between devices, flip(): lax.ppermute(plain(x), axis, [(i, i ^ bit) for i in range(lax.axis_size(a...  77.1 us
    dot_general x17, matrix products, dot(): lax.dot_general(a, b, ((dims[:1], dims[1:]), ((), ())), preferred_element...  61.4 us
    pallas_call x2, Pallas kernels, attend_back(): pl.pallas_call(functools.partial(attend_back_kernel, tile, first, steps),...  33.6 us
    unnamed x213, local copies, waits for them, and re-layouts  23.4 us
    pallas_call x10, Pallas kernels, call(): pl.pallas_call(kernel, grid_spec=pltpu.PrefetchScalarGridSpec(num_scalar_...  23.2 us
    convert_element_type x8, other arithmetic, total(): return (a.astype(F32) + b.astype(F32)).astype(BF16)  14.5 us
    pallas_call x2, Pallas kernels, project(): pl.pallas_call(project_kernel, grid_spec=pltpu.PrefetchScalarGridSpec(num...  11.9 us
  transfers between devices with their start and end apart: 62, of which 26 were waited for; matrix products, arithmetic and copies ran while one was open for 24% of the time, Pallas kernels for 15%

commit v1 on v0

--- a/solution.py
+++ b/solution.py
@@ -715,11 +715,14 @@
     )
 
 
-def finish_kernel(terms_ref, sent_ref, hidden_ref, dy_ref, gain_ref, mixed_ref, grad_ref, sum_ref):
+def finish_kernel(stays, terms_ref, sent_ref, hidden_ref, own_ref, moved_ref, gain_ref,
+                  mixed_ref, grad_ref, dy_ref, sum_ref):
     down = terms_ref[...] + sent_ref[...].astype(F32)
     hat, scale = normalized(down)
     gain = gain_ref[3:4, :]
-    dy = dy_ref[...].astype(F32)
+    low = jnp.where(stays[0] == 1, own_ref[...], moved_ref[...])
+    dy_ref[...] = low
+    dy = low.astype(F32)
     mixed_ref[...] = (hidden_ref[...] + hat * gain).astype(BF16)
     grad_ref[...] = normalized_back(hat, scale, dy * gain).astype(BF16)
 
@@ -730,18 +733,19 @@
     sum_ref[...] += jnp.sum(dy * hat, axis=0, keepdims=True)
 
 
-def finish(terms, sent, hidden, dy, gains):
+def finish(stays, terms, sent, hidden, own, moved, gains):
     total, width = terms.shape
     rows = total // 2
-    row = pl.BlockSpec((rows, width), lambda i: (i, 0))
+    row = pl.BlockSpec((rows, width), lambda i, s: (i, 0))
     return call(
-        finish_kernel, "finish", (2,), [],
-        [row, row, row, row, fixed(*gains.shape)],
+        finish_kernel, "finish", (2,), [stays],
+        [row] * 5 + [fixed(*gains.shape)],
         [
             (shaped(BF16, total, width), row), (shaped(BF16, total, width), row),
+            (shaped(BF16, total, width), row),
             (shaped(F32, 1, width), fixed(1, width)),
         ],
-        5, terms, sent, hidden, dy, gains,
+        5, terms, sent, hidden, own, moved, gains,
     )
 
 
@@ -1283,8 +1287,10 @@
     down_full = join_all(*down_pair, *all_after(down_far, act))
     sent = flip(dot(act[own:], down_full, (1, 1)).astype(BF16), "core", 1)
     terms = dot(act[:own], down_full, (1, 1))
-    dy = settled(cotangent, dy_moved)
-    mixed, grad_down, gain_four = finish(terms, sent, hidden, dy, gains)
+    stays = ((core == 1) == (z >= cp_count // 2)).astype(jnp.int32).reshape(1)
+    mixed, grad_down, dy, gain_four = finish(
+        stays, terms, sent, hidden, cotangent, dy_moved, gains
+    )
     grad_down = jnp.concatenate([grad_down, flip(grad_down, "core", 1)])
 
     x_bit, y_bit = xy & 1, xy >> 1

time: 486 us -> 491 us (1.010)
  Pallas kernels: 80.2 us -> 94.3 us
  starting transfers between devices: 86.3 us -> 74.2 us
    ppermute x54, starting transfers between devices: 77.1 us -> 65 us  [flip(): lax.ppermute(plain(x), axis, [(i, i ^ bit) for i in range(lax.axis_size(a...]
    pallas_call x2, Pallas kernels: 33.6 us -> 42.9 us  [attend_back(): pl.pallas_call(functools.partial(attend_back_kernel, tile, first, steps),...]
  transfers between devices with their start and end apart: 62 -> 62, of which waited for: 26 -> 25; matrix products, arithmetic and copies ran while one was open for 24% -> 25% of each run, Pallas kernels for 15% -> 18%
where the time goes in v1:
time: 491 us; the launch traced here: 484 us
  waiting for transfers between devices  129 us (26%)
  Pallas kernels  94.3 us (19%)
  starting transfers between devices  74.2 us (15%)
  matrix products  65.3 us (13%)
  other arithmetic  65.2 us (13%)
  local copies, waits for them, and re-layouts  40.1 us (8%)
  between operations  16.2 us (3%)
    ppermute x54, waiting for transfers between devices, flip(): lax.ppermute(plain(x), axis, [(i, i ^ bit) for i in range(lax.axis_size(a...  120 us
    dot_general x17, matrix products, dot(): lax.dot_general(a, b, ((dims[:1], dims[1:]), ((), ())), preferred_element...  65.3 us
    ppermute x54, starting transfers between devices, flip(): lax.ppermute(plain(x), axis, [(i, i ^ bit) for i in range(lax.axis_size(a...  65 us
    pallas_call x2, Pallas kernels, attend_back(): pl.pallas_call(functools.partial(attend_back_kernel, tile, first, steps),...  42.9 us
    pallas_call x10, Pallas kernels, call(): pl.pallas_call(kernel, grid_spec=pltpu.PrefetchScalarGridSpec(num_scalar_...  24.7 us
    unnamed x213, local copies, waits for them, and re-layouts  24.3 us
    convert_element_type x8, other arithmetic, total(): return (a.astype(F32) + b.astype(F32)).astype(BF16)  14.5 us
    pallas_call x1, other arithmetic, attend(): pl.pallas_call(functools.partial(attend_kernel, tile), grid_spec=grid_spe...  14.5 us
  transfers between devices with their start and end apart: 62, of which 25 were waited for; matrix products, arithmetic and copies ran while one was open for 25% of the time, Pallas kernels for 18%

profile of v1, /device:TPU:0, one launch (start us, length us, event | category | flops | bytes accessed | tf_op | source)
XLA Modules:
  0.0 484.1 jit_solution(17628207624940593186)
XLA Ops:
  8.3 4.1 collective-permute-start
  16.5 6.0 %collective-permute-done = bf16[144,768]{1,0:T(8,128)(2,1)S(1)} collective-permute-done((bf16[144,768]{1,0:T(8,128)(2,1)S(1)}, bf16[144,768]{1,0:T(8,128)(2,1)S(1)}, u32[]{:S(2)}, u32[]{:S(2)}) %collective-permute-start) | collective-permute-done | bytes 221216 | tf_op jit(solution)/shard_map/ppermute | solution.py:1024
  30.4 3.1 collective-permute-done.4
  35.6 7.0 %collective-permute-start.9 = (bf16[144,768]{1,0:T(8,128)(2,1)S(1)}, bf16[144,768]{1,0:T(8,128)(2,1)S(1)}, u32[]{:S(2)}, u32[]{:S(2)}) collective-permute-start(bf16[144,768]{1,0:T(8,128)(2,1)S(1)} %pad_maximum_fusion.21), channel_id=1, source_target_pairs={{0,4},{4,0},{1,5},{5,1},{2,6},{6,2},{3,7},{7,3},{8,12},{12,8},{9,1... | collective-permute-start | bytes 663560 | tf_op jit(solution)/shard_map/ppermute | solution.py:1024
  42.8 5.1 %collective-permute-start.6 = (bf16[128,256]{1,0:T(8,128)(2,1)S(1)}, bf16[128,256]{1,0:T(8,128)(2,1)}, u32[]{:S(2)}, u32[]{:S(2)}) collective-permute-start(bf16[128,256]{1,0:T(8,128)(2,1)S(1)} %copy-done.88), channel_id=1, source_target_pairs={{0,2},{1,3},{2,0},{3,1},{4,6},{5,7},{6,4},{7,5},{8,10},{9,11},{10,... | collective-permute-start | bytes 196616 | tf_op jit(solution)/shard_map/ppermute | solution.py:1024
  51.9 3.3 collective-permute-done.10
  60.9 5.6 %collective-permute-done.11 = bf16[2,2,144,384]{3,2,1,0:T(8,128)(2,1)S(1)} collective-permute-done((bf16[2,2,144,384]{3,2,1,0:T(8,128)(2,1)S(1)}, bf16[2,2,144,384]{3,2,1,0:T(8,128)(2,1)S(1)}, u32[]{:S(2)}, u32[]{:S(2)}) %collective-permute-start.11) | collective-permute-done | bytes 442400 | tf_op jit(solution)/shard_map/ppermute | solution.py:1024
  73.9 6.2 %project.2 = (bf16[2048,256]{1,0:T(8,128)(2,1)S(1)}, bf16[2048,256]{1,0:T(8,128)(2,1)S(1)}, bf16[2048,256]{1,0:T(8,128)(2,1)S(1)}, bf16[8,256,1024]{2,1,0:T(8,128)(2,1)S(1)}) custom-call(s32[4]{0:T(128)S(1)} %gather_fusion.1, s32[4]{0:T(128)S(1)} %copy-done.65, bf16[2,256,1024]{2,1,0:T(8,128)(2,1)} %bitcast_select_fusion.near.x_ref, ...), custom_call_target="tpu_custom_call" | custom-call | flops 70000000 | bytes 1024 | tf_op jit(solution)/shard_map/project/pallas_call | solution.py:660
  80.2 9.5 %collective-permute-done.7 = bf16[256,512]{1,0:T(8,128)(2,1)S(1)} collective-permute-done((bf16[256,512]{1,0:T(8,128)(2,1)S(1)}, bf16[256,512]{1,0:T(8,128)(2,1)S(1)}, u32[]{:S(2)}, u32[]{:S(2)}) %collective-permute-start.7) | collective-permute-done | bytes 262176 | tf_op jit(solution)/shard_map/ppermute | solution.py:1024
  95.9 5.7 %project.3 = (bf16[2048,256]{1,0:T(8,128)(2,1)S(1)}, bf16[2048,256]{1,0:T(8,128)(2,1)S(1)}, bf16[2048,256]{1,0:T(8,128)(2,1)S(1)}, bf16[8,256,1024]{2,1,0:T(8,128)(2,1)S(1)}) custom-call(s32[4]{0:T(128)S(1)} %gather_fusion, s32[4]{0:T(128)S(1)} %copy-done.66, ...), custom_call_target="tpu_custom_call", output_to_operand_aliasing={{0}: (8, {}), {1}: (9, {}), {2}: (10, {}), {3}: (11, {})} | custom-call | flops 70000000 | bytes 1024 | tf_op jit(solution)/shard_map/project/pallas_call | solution.py:660
  103.6 7.2 %collective-permute-done.17 = bf16[256,512]{1,0:T(8,128)(2,1)S(1)} collective-permute-done((bf16[256,512]{1,0:T(8,128)(2,1)}, bf16[256,512]{1,0:T(8,128)(2,1)S(1)}, u32[]{:S(2)}, u32[]{:S(2)}) %collective-permute-start.17) | collective-permute-done | bytes 262176 | tf_op jit(solution)/shard_map/ppermute | solution.py:1024
  120.2 13.4 %attend.2 = (f32[2048,128]{1,0:T(8,128)S(1)}, bf16[8,256,128]{2,1,0:T(8,128)(2,1)S(1)}, f32[1,2,2048]{2,1,0:T(2,128)S(1)}) custom-call(s32[4,4]{1,0:T(4,128)S(1)} %pad_add_fusion.bounds, s32[8]{0:T(128)S(1)} %convert_add_fusion.6.slot_of, bf16[2048,256]{1,0:T(8,128)(2,1)S(1)} %copy-done.7, bf16[2048,256]{1,0:T(8,128)(2,1)S(1)} %copy-done.11, ...), custom_call_target="tpu_custom_call" | custom-call | flops 140000000 | bytes 1024 | tf_op jit(solution)/shard_map/attend/pallas_call | solution.py:427
  133.8 2.6 collective-permute-done.20
  138.9 14.5 %attend.3 = (f32[2,2,2048]{2,1,0:T(2,128)S(1)}, bf16[8,256,128]{2,1,0:T(8,128)(2,1)S(1)}, f32[2048,128]{1,0:T(8,128)}) fusion(f32[2,2,2048]{2,1,0:T(2,128)S(1)} %constant_dynamic-update-slice_fusion.21, s32[4,4]{1,0:T(4,128)S(1)} %pad_add_fusion.bounds, s32[8]{0:T(128)S(1)} %convert_add_fusion.6.slot_of, bf16[2048,256]{1,0:T(8,128)(2,1)S(1)} %copy-done.7, ...), kind=kCustom, calls=%fused_computation.239 | custom fusion | flops 140000000 | bytes 5802496 | tf_op jit(solution)/shard_map/attend/pallas_call | solution.py:427
  159.1 3.8 collective-permute-done.24.far
  162.9 4.7 collective-permute-done.25.both
  167.6 3.7 mix.1
  174.8 3.0 collective-permute-start.29
  181.5 11.8 %add_convert_fusion = (bf16[1024,2048]{1,0:T(8,128)(2,1)}, bf16[1024,2048]{1,0:T(8,128)(2,1)S(1)}) fusion(bf16[1024,1024]{1,0:T(8,128)(2,1)} %constant_dynamic-update-slice_fusion.14, bf16[1024,2048]{1,0:T(8,128)(2,1)} %all-gather.2.cloned.1.call-done), kind=kOutput, calls=%fused_computation.3 | convolution fusion | flops 4330618880 | bytes 14680064 | tf_op jit(solution)/shard_map/dot_general | solution.py:1072
  193.2 6.9 %collective-permute-done.28 = bf16[2,128,2048]{2,1,0:T(8,128)(2,1)} collective-permute-done((bf16[2,128,2048]{2,1,0:T(8,128)(2,1)}, bf16[2,128,2048]{2,1,0:T(8,128)(2,1)}, u32[]{:S(2)}, u32[]{:S(2)}) %collective-permute-start.28) | collective-permute-done | bytes 1048608 | tf_op jit(solution)/shard_map/ppermute | solution.py:1024
  205.3 3.4 fusion.13
  208.7 5.3 %fusion.7.terms_ref = f32[512,1024]{1,0:T(8,128)S(1)} fusion(bf16[1024,2048]{1,0:T(8,128)(2,1)} %bitcast.299, bf16[1024,2048]{1,0:T(8,128)(2,1)} %copy-done.95), kind=kOutput, calls=%fused_computation.29 | convolution fusion | flops 2147483648 | bytes 8388608 | tf_op jit(solution)/shard_map/dot_general | solution.py:1072
  214.1 4.2 finish.1
  223.8 5.1 %convolution_convert_fusion.1.refs_1_.refs_3_.refs_5_.refs_7_ = bf16[1024,2048]{1,0:T(8,128)(2,1)S(1)} fusion(bf16[1024,1024]{1,0:T(8,128)(2,1)S(1)} %constant_dynamic-update-slice_fusion.16, bf16[1024,2048]{1,0:T(8,128)(2,1)S(1)} %copy-done.96), kind=kOutput, calls=%fused_computation.10 | convolution fusion | flops 4297064448 | bytes 10485760 | tf_op jit(solution)/shard_map/dot_general | solution.py:1072
  228.9 6.6 %multiply_convert_fusion = bf16[1024,2048]{1,0:T(8,128)(2,1)S(1)} fusion(bf16[1024,2048]{1,0:T(8,128)(2,1)} %get-tuple-element.198, bf16[1024,1024]{1,0:T(8,128)(2,1)S(1)} %constant_dynamic-update-slice_fusion.16, bf16[1024,2048]{1,0:T(8,128)(2,1)S(1)} %bitcast.300), kind=kOutput, calls=%fused_computation.2 | convolution fusion | flops 4301258752 | bytes 14680064 | tf_op jit(solution)/shard_map/dot_general | solution.py:1072
  235.5 2.4 fusion.16
  238.3 6.4 %convolution_convert_fusion.refs_0_.refs_2_.refs_4_.refs_6_ = bf16[1024,2048]{1,0:T(8,128)(2,1)S(1)} fusion(bf16[1024,1024]{1,0:T(8,128)(2,1)} %constant_dynamic-update-slice_fusion.14, bf16[1024,2048]{1,0:T(8,128)(2,1)S(1)} %multiply_convert_fusion), kind=kOutput, calls=%fused_computation.9 | convolution fusion | flops 4297064448 | bytes 10485760 | tf_op jit(solution)/shard_map/dot_general | solution.py:1072
  244.8 2.7 cut_lines.1
  255.3 4.4 turn.1
  264.6 3.9 collective-permute-done.36
  268.5 5.1 %collective-permute-done.34 = bf16[2,256,256]{2,1,0:T(8,128)(2,1)S(1)} collective-permute-done((bf16[2,256,256]{2,1,0:T(8,128)(2,1)S(1)}, bf16[2,256,256]{2,1,0:T(8,128)(2,1)S(1)}, u32[]{:S(2)}, u32[]{:S(2)}) %collective-permute-start.34) | collective-permute-done | bytes 262176 | tf_op jit(solution)/shard_map/ppermute | solution.py:1024
  284.2 28.3 %attend_back.2 = (bf16[4,256,768]{2,1,0:T(8,128)(2,1)S(1)}, f32[2,128,1024]{2,1,0:T(8,128)S(1)}) custom-call(s32[4,4]{1,0:T(4,128)S(1)} %pad_add_fusion.bounds, s32[8]{0:T(128)S(1)} %convert_add_fusion.6.slot_of, bf16[2048,256]{1,0:T(8,128)(2,1)S(1)} %copy-done.8, bf16[2048,256]{1,0:T(8,128)(2,1)S(1)} %copy-done.12, bf16[2048,256]{1,0:T(8,128)(2,1)S(1)} %copy-done.16, ...), custom_call_target="tpu_custom_call" | custom-call | flops 230000000 | bytes 1024 | tf_op jit(solution)/shard_map/attend_back/pallas_call | solution.py:573
  316.7 2.7 collective-permute-start.41
  322.0 2.5 add_convert_fusion.6
  324.8 2.6 fusion.20
  327.5 2.5 fusion.21
  334.9 3.6 fusion.90
  340.5 14.6 %attend_back.3 = bf16[4,256,768]{2,1,0:T(8,128)(2,1)S(1)} custom-call(s32[4,4]{1,0:T(4,128)S(1)} %pad_add_fusion.bounds, s32[8]{0:T(128)S(1)} %convert_add_fusion.6.slot_of, bf16[2048,256]{1,0:T(8,128)(2,1)S(1)} %copy-done.9, bf16[2048,256]{1,0:T(8,128)(2,1)S(1)} %copy-done.13, bf16[2048,256]{1,0:T(8,128)(2,1)S(1)} %copy-done.17, ...), custom_call_target="tpu_custom_call" | custom-call | flops 230000000 | bytes 1024 | tf_op jit(solution)/shard_map/attend_back/pallas_call | solution.py:573
  358.5 3.4 multiply_reduce_fusion
  366.0 2.6 add_convert_fusion.5
  368.6 2.8 convert_add_fusion.2.keep_ref
  371.4 3.4 spread_first.1
  379.4 15.4 %collective-permute-done.49.low_far = bf16[2,11,128,128]{3,2,1,0:T(8,128)(2,1)} collective-permute-done((bf16[2,11,128,128]{3,2,1,0:T(8,128)(2,1)}, bf16[2,11,128,128]{3,2,1,0:T(8,128)(2,1)}, u32[]{:S(2)}, u32[]{:S(2)}) %collective-permute-start.49) | collective-permute-done | bytes 720928 | tf_op jit(solution)/shard_map/ppermute | solution.py:1024
  397.2 3.0 spread_second.1
  411.3 10.9 %collective-permute-done.51.low_far = bf16[11,128,128]{2,1,0:T(8,128)(2,1)S(1)} collective-permute-done((bf16[11,128,128]{2,1,0:T(8,128)(2,1)}, bf16[11,128,128]{2,1,0:T(8,128)(2,1)S(1)}, u32[]{:S(2)}, u32[]{:S(2)}) %collective-permute-start.51) | collective-permute-done | bytes 360480 | tf_op jit(solution)/shard_map/ppermute | solution.py:1024
  423.0 12.1 %collective-permute-start.56 = (bf16[11,128,128]{2,1,0:T(8,128)(2,1)S(1)}, bf16[11,128,128]{2,1,0:T(8,128)(2,1)S(1)}, u32[]{:S(2)}, u32[]{:S(2)}) collective-permute-start(bf16[11,128,128]{2,1,0:T(8,128)(2,1)S(1)} %get-tuple-element.258), channel_id=1, source_target_pairs={{0,2},{1,3},{2,0},{3,1},{4,6},{5,7},{6,4},{7,5},{8,10},{9,11},{10,... | collective-permute-start | bytes 1081352 | tf_op jit(solution)/shard_map/ppermute | solution.py:1024
  438.6 21.9 %collective-permute-done.56.far = bf16[11,128,128]{2,1,0:T(8,128)(2,1)S(1)} collective-permute-done((bf16[11,128,128]{2,1,0:T(8,128)(2,1)S(1)}, bf16[11,128,128]{2,1,0:T(8,128)(2,1)S(1)}, u32[]{:S(2)}, u32[]{:S(2)}) %collective-permute-start.56) | collective-permute-done | bytes 360480 | tf_op jit(solution)/shard_map/ppermute | solution.py:1024
  461.3 9.1 %collective-permute-done.59 = bf16[448,512]{1,0:T(8,128)(2,1)S(1)} collective-permute-done((bf16[448,512]{1,0:T(8,128)(2,1)S(1)}, bf16[448,512]{1,0:T(8,128)(2,1)S(1)}, u32[]{:S(2)}, u32[]{:S(2)}) %collective-permute-start.59) | collective-permute-done | bytes 458784 | tf_op jit(solution)/shard_map/ppermute | solution.py:1024
  (469 shorter events, 149.8 us)
Async XLA Ops:
  7.2 174.3 %all-gather.2.cloned.1.call-start = ((), (), s32[]{:S(2)}) async-start(), calls=%async_computation | async-start | bytes 5242880 | tf_op jit(solution)/shard_map/all_gather | solution.py:1254
  8.3 14.3 %collective-permute-start = (bf16[144,768]{1,0:T(8,128)(2,1)S(1)}, bf16[144,768]{1,0:T(8,128)(2,1)S(1)}, u32[]{:S(2)}, u32[]{:S(2)}) collective-permute-start(bf16[144,768]{1,0:T(8,128)(2,1)S(1)} %fusion.57), channel_id=1, source_target_pairs={{0,2},{1,3},{2,0},{3,1},{4,6},{5,7},{6,4},{7,5},{8,10},{9,11},{10,... | collective-permute-start | bytes 663560 | tf_op jit(solution)/shard_map/ppermute | solution.py:1024
  22.8 35.8 %collective-permute-start.2 = (bf16[2,256,1024]{2,1,0:T(8,128)(2,1)}, bf16[2,256,1024]{2,1,0:T(8,128)(2,1)}, u32[]{:S(2)}, u32[]{:S(2)}) collective-permute-start(bf16[2,256,1024]{2,1,0:T(8,128)(2,1)} %bitcast.6), channel_id=1, source_target_pairs={{4,2},{2,4},{5,3},{3,5},{12,10},{10,12},{13,11},{11,13},{20,18},{1... | collective-permute-start | bytes 3145736 | tf_op jit(solution)/shard_map/ppermute | solution.py:1034
  35.6 12.3 %collective-permute-start.9 = (bf16[144,768]{1,0:T(8,128)(2,1)S(1)}, bf16[144,768]{1,0:T(8,128)(2,1)S(1)}, u32[]{:S(2)}, u32[]{:S(2)}) collective-permute-start(bf16[144,768]{1,0:T(8,128)(2,1)S(1)} %pad_maximum_fusion.21), channel_id=1, source_target_pairs={{0,4},{4,0},{1,5},{5,1},{2,6},{6,2},{3,7},{7,3},{8,12},{12,8},{9,1... | collective-permute-start | bytes 663560 | tf_op jit(solution)/shard_map/ppermute | solution.py:1024
  42.7 8.4 %collective-permute-start.5 = (bf16[2,128,512]{2,1,0:T(8,128)(2,1)S(1)}, bf16[2,128,512]{2,1,0:T(8,128)(2,1)S(1)}, u32[]{:S(2)}, u32[]{:S(2)}) collective-permute-start(bf16[2,128,512]{2,1,0:T(8,128)(2,1)S(1)} %pad_maximum_fusion.25), channel_id=1, source_target_pairs={{0,4},{4,0},{1,5},{5,1},{2,6},{6,2},{3,7},{7,3},{8,12},{12,8},{9,1... | collective-permute-start | bytes 786440 | tf_op jit(solution)/shard_map/ppermute | solution.py:1024
  42.8 25.9 %collective-permute-start.6 = (bf16[128,256]{1,0:T(8,128)(2,1)S(1)}, bf16[128,256]{1,0:T(8,128)(2,1)}, u32[]{:S(2)}, u32[]{:S(2)}) collective-permute-start(bf16[128,256]{1,0:T(8,128)(2,1)S(1)} %copy-done.88), channel_id=1, source_target_pairs={{0,2},{1,3},{2,0},{3,1},{4,6},{5,7},{6,4},{7,5},{8,10},{9,11},{10,... | collective-permute-start | bytes 196616 | tf_op jit(solution)/shard_map/ppermute | solution.py:1024
  55.3 11.2 %collective-permute-start.11 = (bf16[2,2,144,384]{3,2,1,0:T(8,128)(2,1)S(1)}, bf16[2,2,144,384]{3,2,1,0:T(8,128)(2,1)S(1)}, u32[]{:S(2)}, u32[]{:S(2)}) collective-permute-start(bf16[2,2,144,384]{3,2,1,0:T(8,128)(2,1)S(1)} %pad_maximum_fusion.19), channel_id=1, source_target_pairs={{0,16},{8,24},{16,0},{24,8},{1,17},{9,25},{17,1},{25,9},{2,18},{10... | collective-permute-start | bytes 1327112 | tf_op jit(solution)/shard_map/ppermute | solution.py:1024
  57.0 10.8 %collective-permute-start.13 = (bf16[2,2,144,384]{3,2,1,0:T(8,128)(2,1)S(1)}, bf16[2,2,144,384]{3,2,1,0:T(8,128)(2,1)S(1)}, u32[]{:S(2)}, u32[]{:S(2)}) collective-permute-start(bf16[2,2,144,384]{3,2,1,0:T(8,128)(2,1)S(1)} %pad_maximum_fusion.20), channel_id=1, source_target_pairs={{0,8},{8,0},{16,24},{24,16},{1,9},{9,1},{17,25},{25,17},{2,10},{10... | collective-permute-start | bytes 1327112 | tf_op jit(solution)/shard_map/ppermute | solution.py:1024
  60.9 31.1 %collective-permute-start.3 = (bf16[2,256,1024]{2,1,0:T(8,128)(2,1)}, bf16[2,256,1024]{2,1,0:T(8,128)(2,1)}, u32[]{:S(2)}, u32[]{:S(2)}) collective-permute-start(bf16[2,256,1024]{2,1,0:T(8,128)(2,1)} %bitcast_select_fusion.near.x_ref), channel_id=1, source_target_pairs={{0,1},{1,0},{2,3},{3,2},{4,5},{5,4},{6,7},{7,6},{8,9},{9,8},{10,11... | collective-permute-start | bytes 3145736 | tf_op jit(solution)/shard_map/ppermute | solution.py:1024
  60.9 11.6 %collective-permute-start.8 = (bf16[2,256,1024]{2,1,0:T(8,128)(2,1)}, bf16[2,256,1024]{2,1,0:T(8,128)(2,1)}, u32[]{:S(2)}, u32[]{:S(2)}) collective-permute-start(bf16[2,256,1024]{2,1,0:T(8,128)(2,1)} %bitcast_select_fusion.near.x_ref), channel_id=1, source_target_pairs={{0,4},{4,0},{1,5},{5,1},{2,6},{6,2},{3,7},{7,3},{8,12},{12,8},{9,1... | collective-permute-start | bytes 3145736 | tf_op jit(solution)/shard_map/ppermute | solution.py:1024
  68.7 20.9 %collective-permute-start.7 = (bf16[256,512]{1,0:T(8,128)(2,1)S(1)}, bf16[256,512]{1,0:T(8,128)(2,1)S(1)}, u32[]{:S(2)}, u32[]{:S(2)}) collective-permute-start(bf16[256,512]{1,0:T(8,128)(2,1)S(1)} %get-tuple-element.161), channel_id=1, source_target_pairs={{0,2},{1,3},{2,0},{3,1},{4,6},{5,7},{6,4},{7,5},{8,10},{9,11},{10,... | collective-permute-start | bytes 786440 | tf_op jit(solution)/shard_map/ppermute | solution.py:1024
  71.2 22.1 %collective-permute-start.15 = (bf16[128,512]{1,0:T(8,128)(2,1)S(1)}, bf16[128,512]{1,0:T(8,128)(2,1)S(1)}, u32[]{:S(2)}, u32[]{:S(2)}) collective-permute-start(bf16[128,512]{1,0:T(8,128)(2,1)S(1)} %pad_maximum_fusion.28), channel_id=1, source_target_pairs={{0,1},{1,0},{2,3},{3,2},{4,5},{5,4},{6,7},{7,6},{8,9},{9,8},{10,11... | collective-permute-start | bytes 393224 | tf_op jit(solution)/shard_map/ppermute | solution.py:1024
  93.4 18.7 %collective-permute-start.16 = (bf16[256,1024]{1,0:T(8,128)(2,1)S(1)}, bf16[256,1024]{1,0:T(8,128)(2,1)S(1)}, u32[]{:S(2)}, u32[]{:S(2)}) collective-permute-start(bf16[256,1024]{1,0:T(8,128)(2,1)S(1)} %pad_maximum_fusion.13), channel_id=1, source_target_pairs={{0,1},{1,0},{2,3},{3,2},{4,5},{5,4},{6,7},{7,6},{8,9},{9,8},{10,11... | collective-permute-start | bytes 1572872 | tf_op jit(solution)/shard_map/ppermute | solution.py:1024
  93.7 17.1 %collective-permute-start.17 = (bf16[256,512]{1,0:T(8,128)(2,1)}, bf16[256,512]{1,0:T(8,128)(2,1)S(1)}, u32[]{:S(2)}, u32[]{:S(2)}) collective-permute-start(bf16[256,512]{1,0:T(8,128)(2,1)} %get-tuple-element.170), channel_id=1, source_target_pairs={{0,2},{1,3},{2,0},{3,1},{4,6},{5,7},{6,4},{7,5},{8,10},{9,11},{10,... | collective-permute-start | bytes 786440 | tf_op jit(solution)/shard_map/ppermute | solution.py:1024
  95.0 15.8 %collective-permute-start.18 = (bf16[1,128,1024]{2,1,0:T(8,128)(2,1)S(1)}, bf16[1,128,1024]{2,1,0:T(8,128)(2,1)S(1)}, u32[]{:S(2)}, u32[]{:S(2)}) collective-permute-start(bf16[1,128,1024]{2,1,0:T(8,128)(2,1)S(1)} %maximum_bitcast_fusion.2), channel_id=1, source_target_pairs={{0,8},{8,0},{16,24},{24,16},{1,9},{9,1},{17,25},{25,17},{2,10},{10... | collective-permute-start | bytes 786440 | tf_op jit(solution)/shard_map/ppermute | solution.py:1024
  114.2 19.6 %collective-permute-start.19 = (bf16[256,1024]{1,0:T(8,128)(2,1)}, bf16[256,1024]{1,0:T(8,128)(2,1)}, u32[]{:S(2)}, u32[]{:S(2)}) collective-permute-start(bf16[256,1024]{1,0:T(8,128)(2,1)} %pad_maximum_fusion.15), channel_id=1, source_target_pairs={{0,1},{1,0},{2,3},{3,2},{4,5},{5,4},{6,7},{7,6},{8,9},{9,8},{10,11... | collective-permute-start | bytes 1572872 | tf_op jit(solution)/shard_map/ppermute | solution.py:1024
  118.1 18.2 %collective-permute-start.20 = (bf16[2,128,1024]{2,1,0:T(8,128)(2,1)S(1)}, bf16[2,128,1024]{2,1,0:T(8,128)(2,1)S(1)}, u32[]{:S(2)}, u32[]{:S(2)}) collective-permute-start(bf16[2,128,1024]{2,1,0:T(8,128)(2,1)S(1)} %pad_maximum_fusion.14), channel_id=1, source_target_pairs={{0,16},{8,24},{16,0},{24,8},{1,17},{9,25},{17,1},{25,9},{2,18},{10... | collective-permute-start | bytes 1572872 | tf_op jit(solution)/shard_map/ppermute | solution.py:1024
  138.0 17.6 %collective-permute-start.21 = (bf16[1,128,2048]{2,1,0:T(8,128)(2,1)S(1)}, bf16[1,128,2048]{2,1,0:T(8,128)(2,1)S(1)}, u32[]{:S(2)}, u32[]{:S(2)}) collective-permute-start(bf16[1,128,2048]{2,1,0:T(8,128)(2,1)S(1)} %get-tuple-element.183), channel_id=1, source_target_pairs={{0,8},{8,0},{16,24},{24,16},{1,9},{9,1},{17,25},{25,17},{2,10},{10... | collective-permute-start | bytes 1572872 | tf_op jit(solution)/shard_map/ppermute | solution.py:1024
  138.0 17.9 %collective-permute-start.22 = (bf16[1,128,2048]{2,1,0:T(8,128)(2,1)S(1)}, bf16[1,128,2048]{2,1,0:T(8,128)(2,1)S(1)}, u32[]{:S(2)}, u32[]{:S(2)}) collective-permute-start(bf16[1,128,2048]{2,1,0:T(8,128)(2,1)S(1)} %get-tuple-element.185), channel_id=1, source_target_pairs={{0,16},{8,24},{16,0},{24,8},{1,17},{9,25},{17,1},{25,9},{2,18},{10... | collective-permute-start | bytes 1572872 | tf_op jit(solution)/shard_map/ppermute | solution.py:1024
  153.7 9.2 %collective-permute-start.24 = (bf16[2,256,256]{2,1,0:T(8,128)(2,1)S(1)}, bf16[2,256,256]{2,1,0:T(8,128)(2,1)S(1)}, u32[]{:S(2)}, u32[]{:S(2)}) collective-permute-start(bf16[2,256,256]{2,1,0:T(8,128)(2,1)S(1)} %get-tuple-element.343), channel_id=1, source_target_pairs={{0,1},{1,0},{2,3},{3,2},{4,5},{5,4},{6,7},{7,6},{8,9},{9,8},{10,11... | collective-permute-start | bytes 786440 | tf_op jit(solution)/shard_map/ppermute | solution.py:1024
  153.8 13.8 %collective-permute-start.25 = (bf16[2,256,256]{2,1,0:T(8,128)(2,1)S(1)}, bf16[2,256,256]{2,1,0:T(8,128)(2,1)S(1)}, u32[]{:S(2)}, u32[]{:S(2)}) collective-permute-start(bf16[2,256,256]{2,1,0:T(8,128)(2,1)S(1)} %get-tuple-element.342), channel_id=1, source_target_pairs={{0,5},{1,4},{2,7},{3,6},{4,1},{5,0},{6,3},{7,2},{8,13},{9,12},{10,... | collective-permute-start | bytes 786440 | tf_op jit(solution)/shard_map/ppermute | solution.py:1066
  174.8 25.4 %collective-permute-start.28 = (bf16[2,128,2048]{2,1,0:T(8,128)(2,1)}, bf16[2,128,2048]{2,1,0:T(8,128)(2,1)}, u32[]{:S(2)}, u32[]{:S(2)}) collective-permute-start(bf16[2,128,2048]{2,1,0:T(8,128)(2,1)} %pad_maximum_fusion.8), channel_id=1, source_target_pairs={{0,16},{8,24},{16,0},{24,8},{1,17},{9,25},{17,1},{25,9},{2,18},{10... | collective-permute-start | bytes 3145736 | tf_op jit(solution)/shard_map/ppermute | solution.py:1024
  174.8 26.3 %collective-permute-start.29 = (bf16[2,1,128,2048]{3,2,1,0:T(8,128)(2,1)}, bf16[2,1,128,2048]{3,2,1,0:T(8,128)(2,1)}, u32[]{:S(2)}, u32[]{:S(2)}) collective-permute-start(bf16[2,1,128,2048]{3,2,1,0:T(8,128)(2,1)} %maximum_bitcast_fusion.1), channel_id=1, source_target_pairs={{0,8},{8,0},{16,24},{24,16},{1,9},{9,1},{17,25},{25,17},{2,10},{10... | collective-permute-start | bytes 3145736 | tf_op jit(solution)/shard_map/ppermute | solution.py:1024
  177.7 36.3 %collective-permute-start.31 = (bf16[512,1024]{1,0:T(8,128)(2,1)}, bf16[512,1024]{1,0:T(8,128)(2,1)}, u32[]{:S(2)}, u32[]{:S(2)}) collective-permute-start(bf16[512,1024]{1,0:T(8,128)(2,1)} %bitcast.41.own_ref), channel_id=1, source_target_pairs={{4,2},{2,4},{5,3},{3,5},{12,10},{10,12},{13,11},{11,13},{20,18},{1... | collective-permute-start | bytes 3145736 | tf_op jit(solution)/shard_map/ppermute | solution.py:1034
  237.9 16.7 %collective-permute-start.33 = (bf16[512,1024]{1,0:T(8,128)(2,1)S(1)}, bf16[512,1024]{1,0:T(8,128)(2,1)S(1)}, u32[]{:S(2)}, u32[]{:S(2)}) collective-permute-start(bf16[512,1024]{1,0:T(8,128)(2,1)S(1)} %fusion.16), channel_id=1, source_target_pairs={{0,4},{4,0},{1,5},{5,1},{2,6},{6,2},{3,7},{7,3},{8,12},{12,8},{9,1... | collective-permute-start | bytes 3145736 | tf_op jit(solution)/shard_map/ppermute | solution.py:1024
  250.0 62.6 %collective-permute-start.39 = (bf16[2,224,2048]{2,1,0:T(8,128)(2,1)}, bf16[2,224,2048]{2,1,0:T(8,128)(2,1)}, u32[]{:S(2)}, u32[]{:S(2)}) collective-permute-start(bf16[2,224,2048]{2,1,0:T(8,128)(2,1)} %get-tuple-element.199), channel_id=1, source_target_pairs={{0,8},{8,0},{16,24},{24,16},{1,9},{9,1},{17,25},{25,17},{2,10},{10... | collective-permute-start | bytes 5505032 | tf_op jit(solution)/shard_map/ppermute | solution.py:1024
  251.8 60.8 %collective-permute-start.40 = (bf16[2,224,2048]{2,1,0:T(8,128)(2,1)}, bf16[2,224,2048]{2,1,0:T(8,128)(2,1)}, u32[]{:S(2)}, u32[]{:S(2)}) collective-permute-start(bf16[2,224,2048]{2,1,0:T(8,128)(2,1)} %get-tuple-element.200), channel_id=1, source_target_pairs={{0,16},{8,24},{16,0},{24,8},{1,17},{9,25},{17,1},{25,9},{2,18},{10... | collective-permute-start | bytes 5505032 | tf_op jit(solution)/shard_map/ppermute | solution.py:1024
  259.8 8.7 %collective-permute-start.36 = (bf16[2,256,256]{2,1,0:T(8,128)(2,1)S(1)}, bf16[2,256,256]{2,1,0:T(8,128)(2,1)S(1)}, u32[]{:S(2)}, u32[]{:S(2)}) collective-permute-start(bf16[2,256,256]{2,1,0:T(8,128)(2,1)S(1)} %get-tuple-element.339), channel_id=1, source_target_pairs={{0,5},{1,4},{2,7},{3,6},{4,1},{5,0},{6,3},{7,2},{8,13},{9,12},{10,... | collective-permute-start | bytes 786440 | tf_op jit(solution)/shard_map/ppermute | solution.py:1066
  259.9 8.6 %collective-permute-start.35 = (bf16[2,256,256]{2,1,0:T(8,128)(2,1)S(1)}, bf16[2,256,256]{2,1,0:T(8,128)(2,1)S(1)}, u32[]{:S(2)}, u32[]{:S(2)}) collective-permute-start(bf16[2,256,256]{2,1,0:T(8,128)(2,1)S(1)} %get-tuple-element.340), channel_id=1, source_target_pairs={{0,4},{4,0},{1,5},{5,1},{2,6},{6,2},{3,7},{7,3},{8,12},{12,8},{9,1... | collective-permute-start | bytes 786440 | tf_op jit(solution)/shard_map/ppermute | solution.py:1024
  260.3 13.3 %collective-permute-start.34 = (bf16[2,256,256]{2,1,0:T(8,128)(2,1)S(1)}, bf16[2,256,256]{2,1,0:T(8,128)(2,1)S(1)}, u32[]{:S(2)}, u32[]{:S(2)}) collective-permute-start(bf16[2,256,256]{2,1,0:T(8,128)(2,1)S(1)} %get-tuple-element.341), channel_id=1, source_target_pairs={{0,1},{1,0},{2,3},{3,2},{4,5},{5,4},{6,7},{7,6},{8,9},{9,8},{10,11... | collective-permute-start | bytes 786440 | tf_op jit(solution)/shard_map/ppermute | solution.py:1024
  274.7 37.9 %collective-permute-start.37 = (bf16[512,1024]{1,0:T(8,128)(2,1)}, bf16[512,1024]{1,0:T(8,128)(2,1)}, u32[]{:S(2)}, u32[]{:S(2)}) collective-permute-start(bf16[512,1024]{1,0:T(8,128)(2,1)} %get-tuple-element.259), channel_id=1, source_target_pairs={{4,2},{2,4},{5,3},{3,5},{12,10},{10,12},{13,11},{11,13},{20,18},{1... | collective-permute-start | bytes 3145736 | tf_op jit(solution)/shard_map/ppermute | solution.py:1034
  277.3 35.3 %collective-permute-start.38 = (bf16[2,256,512]{2,1,0:T(8,128)(2,1)}, bf16[2,256,512]{2,1,0:T(8,128)(2,1)}, u32[]{:S(2)}, u32[]{:S(2)}) collective-permute-start(bf16[2,256,512]{2,1,0:T(8,128)(2,1)} %get-tuple-element.333), channel_id=1, source_target_pairs={{0,1},{1,0},{2,3},{3,2},{4,5},{5,4},{6,7},{7,6},{8,9},{9,8},{10,11... | collective-permute-start | bytes 1572872 | tf_op jit(solution)/shard_map/ppermute | solution.py:1024
  324.6 30.6 %collective-permute-start.43 = (bf16[4,128,1024]{2,1,0:T(8,128)(2,1)}, bf16[4,128,1024]{2,1,0:T(8,128)(2,1)S(1)}, u32[]{:S(2)}, u32[]{:S(2)}) collective-permute-start(bf16[4,128,1024]{2,1,0:T(8,128)(2,1)} %dynamic-slice_bitcast_fusion), channel_id=1, source_target_pairs={{0,4},{4,0},{1,5},{5,1},{2,6},{6,2},{3,7},{7,3},{8,12},{12,8},{9,1... | collective-permute-start | bytes 3145736 | tf_op jit(solution)/shard_map/ppermute | solution.py:1024
  327.5 27.7 %collective-permute-start.44 = (bf16[224,2048]{1,0:T(8,128)(2,1)}, bf16[224,2048]{1,0:T(8,128)(2,1)}, u32[]{:S(2)}, u32[]{:S(2)}) collective-permute-start(bf16[224,2048]{1,0:T(8,128)(2,1)} %fusion.20), channel_id=1, source_target_pairs={{0,16},{8,24},{16,0},{24,8},{1,17},{9,25},{17,1},{25,9},{2,18},{10... | collective-permute-start | bytes 2752520 | tf_op jit(solution)/shard_map/ppermute | solution.py:1024
  330.0 25.1 %collective-permute-start.45 = (bf16[224,2048]{1,0:T(8,128)(2,1)}, bf16[224,2048]{1,0:T(8,128)(2,1)}, u32[]{:S(2)}, u32[]{:S(2)}) collective-permute-start(bf16[224,2048]{1,0:T(8,128)(2,1)} %fusion.21), channel_id=1, source_target_pairs={{0,8},{8,0},{16,24},{24,16},{1,9},{9,1},{17,25},{25,17},{2,10},{10... | collective-permute-start | bytes 2752520 | tf_op jit(solution)/shard_map/ppermute | solution.py:1024
  332.1 23.0 %collective-permute-start.42 = (bf16[256,512]{1,0:T(8,128)(2,1)S(1)}, bf16[256,512]{1,0:T(8,128)(2,1)S(1)}, u32[]{:S(2)}, u32[]{:S(2)}) collective-permute-start(bf16[256,512]{1,0:T(8,128)(2,1)S(1)} %copy-done.86), channel_id=1, source_target_pairs={{0,2},{1,3},{2,0},{3,1},{4,6},{5,7},{6,4},{7,5},{8,10},{9,11},{10,... | collective-permute-start | bytes 786440 | tf_op jit(solution)/shard_map/ppermute | solution.py:1024
  333.1 22.1 %collective-permute-start.46 = (bf16[256,1024]{1,0:T(8,128)(2,1)}, bf16[256,1024]{1,0:T(8,128)(2,1)S(1)}, u32[]{:S(2)}, u32[]{:S(2)}) collective-permute-start(bf16[256,1024]{1,0:T(8,128)(2,1)} %add_convert_fusion.6), channel_id=1, source_target_pairs={{0,1},{1,0},{2,3},{3,2},{4,5},{5,4},{6,7},{7,6},{8,9},{9,8},{10,11... | collective-permute-start | bytes 1572872 | tf_op jit(solution)/shard_map/ppermute | solution.py:1024
  375.7 19.8 %collective-permute-start.50 = (bf16[2,12,128,128]{3,2,1,0:T(8,128)(2,1)}, bf16[2,12,128,128]{3,2,1,0:T(8,128)(2,1)}, u32[]{:S(2)}, u32[]{:S(2)}) collective-permute-start(bf16[2,12,128,128]{3,2,1,0:T(8,128)(2,1)} %get-tuple-element.250), channel_id=1, source_target_pairs={{0,16},{8,24},{16,0},{24,8},{1,17},{9,25},{17,1},{25,9},{2,18},{10... | collective-permute-start | bytes 2359304 | tf_op jit(solution)/shard_map/ppermute | solution.py:1024
  376.7 18.1 %collective-permute-start.49 = (bf16[2,11,128,128]{3,2,1,0:T(8,128)(2,1)}, bf16[2,11,128,128]{3,2,1,0:T(8,128)(2,1)}, u32[]{:S(2)}, u32[]{:S(2)}) collective-permute-start(bf16[2,11,128,128]{3,2,1,0:T(8,128)(2,1)} %get-tuple-element.248), channel_id=1, source_target_pairs={{0,8},{8,0},{16,24},{24,16},{1,9},{9,1},{17,25},{25,17},{2,10},{10... | collective-permute-start | bytes 2162696 | tf_op jit(solution)/shard_map/ppermute | solution.py:1024
  378.0 27.9 %collective-permute-start.54 = (bf16[256,1024]{1,0:T(8,128)(2,1)S(1)}, bf16[256,1024]{1,0:T(8,128)(2,1)S(1)}, u32[]{:S(2)}, u32[]{:S(2)}) collective-permute-start(bf16[256,1024]{1,0:T(8,128)(2,1)S(1)} %copy-done.37), channel_id=1, source_target_pairs={{4,2},{2,4},{5,3},{3,5},{12,10},{10,12},{13,11},{11,13},{20,18},{1... | collective-permute-start | bytes 1572872 | tf_op jit(solution)/shard_map/ppermute | solution.py:1034
  379.0 27.0 %collective-permute-start.53 = (bf16[256,1024]{1,0:T(8,128)(2,1)}, bf16[256,1024]{1,0:T(8,128)(2,1)S(1)}, u32[]{:S(2)}, u32[]{:S(2)}) collective-permute-start(bf16[256,1024]{1,0:T(8,128)(2,1)} %add_convert_fusion.5), channel_id=1, source_target_pairs={{0,1},{1,0},{2,3},{3,2},{4,5},{5,4},{6,7},{7,6},{8,9},{9,8},{10,11... | collective-permute-start | bytes 1572872 | tf_op jit(solution)/shard_map/ppermute | solution.py:1024
  405.7 29.4 %collective-permute-start.58 = (bf16[2,448,512]{2,1,0:T(8,128)(2,1)}, bf16[2,448,512]{2,1,0:T(8,128)(2,1)}, u32[]{:S(2)}, u32[]{:S(2)}) collective-permute-start(bf16[2,448,512]{2,1,0:T(8,128)(2,1)} %get-tuple-element.325), channel_id=1, source_target_pairs={{0,1},{1,0},{2,3},{3,2},{4,5},{5,4},{6,7},{7,6},{8,9},{9,8},{10,11... | collective-permute-start | bytes 2752520 | tf_op jit(solution)/shard_map/ppermute | solution.py:1024
  407.4 14.8 %collective-permute-start.55 = (bf16[256,1024]{1,0:T(8,128)(2,1)S(1)}, bf16[256,1024]{1,0:T(8,128)(2,1)}, u32[]{:S(2)}, u32[]{:S(2)}) collective-permute-start(bf16[256,1024]{1,0:T(8,128)(2,1)S(1)} %end.3), channel_id=1, source_target_pairs={{4,2},{2,4},{5,3},{3,5},{12,10},{10,12},{13,11},{11,13},{20,18},{1... | collective-permute-start | bytes 1572872 | tf_op jit(solution)/shard_map/ppermute | solution.py:1034
  408.8 13.3 %collective-permute-start.52 = (bf16[12,128,128]{2,1,0:T(8,128)(2,1)}, bf16[12,128,128]{2,1,0:T(8,128)(2,1)S(1)}, u32[]{:S(2)}, u32[]{:S(2)}) collective-permute-start(bf16[12,128,128]{2,1,0:T(8,128)(2,1)} %get-tuple-element.253), channel_id=1, source_target_pairs={{0,8},{8,0},{16,24},{24,16},{1,9},{9,1},{17,25},{25,17},{2,10},{10... | collective-permute-start | bytes 1179656 | tf_op jit(solution)/shard_map/ppermute | solution.py:1024
  410.9 11.3 %collective-permute-start.51 = (bf16[11,128,128]{2,1,0:T(8,128)(2,1)}, bf16[11,128,128]{2,1,0:T(8,128)(2,1)S(1)}, u32[]{:S(2)}, u32[]{:S(2)}) collective-permute-start(bf16[11,128,128]{2,1,0:T(8,128)(2,1)} %get-tuple-element.252), channel_id=1, source_target_pairs={{0,16},{8,24},{16,0},{24,8},{1,17},{9,25},{17,1},{25,9},{2,18},{10... | collective-permute-start | bytes 1081352 | tf_op jit(solution)/shard_map/ppermute | solution.py:1024
  423.0 37.6 %collective-permute-start.56 = (bf16[11,128,128]{2,1,0:T(8,128)(2,1)S(1)}, bf16[11,128,128]{2,1,0:T(8,128)(2,1)S(1)}, u32[]{:S(2)}, u32[]{:S(2)}) collective-permute-start(bf16[11,128,128]{2,1,0:T(8,128)(2,1)S(1)} %get-tuple-element.258), channel_id=1, source_target_pairs={{0,2},{1,3},{2,0},{3,1},{4,6},{5,7},{6,4},{7,5},{8,10},{9,11},{10,... | collective-permute-start | bytes 1081352 | tf_op jit(solution)/shard_map/ppermute | solution.py:1024
  436.2 34.2 %collective-permute-start.59 = (bf16[448,512]{1,0:T(8,128)(2,1)S(1)}, bf16[448,512]{1,0:T(8,128)(2,1)S(1)}, u32[]{:S(2)}, u32[]{:S(2)}) collective-permute-start(bf16[448,512]{1,0:T(8,128)(2,1)S(1)} %fusion.27), channel_id=1, source_target_pairs={{0,2},{1,3},{2,0},{3,1},{4,6},{5,7},{6,4},{7,5},{8,10},{9,11},{10,... | collective-permute-start | bytes 1376264 | tf_op jit(solution)/shard_map/ppermute | solution.py:1024
  461.2 12.6 %collective-permute-start.57 = (bf16[5,128,128]{2,1,0:T(8,128)(2,1)S(1)}, bf16[5,128,128]{2,1,0:T(8,128)(2,1)S(1)}, u32[]{:S(2)}, u32[]{:S(2)}) collective-permute-start(bf16[5,128,128]{2,1,0:T(8,128)(2,1)S(1)} %get-tuple-element.262), channel_id=1, source_target_pairs={{0,1},{1,0},{2,3},{3,2},{4,5},{5,4},{6,7},{7,6},{8,9},{9,8},{10,11... | collective-permute-start | bytes 491528 | tf_op jit(solution)/shard_map/ppermute | solution.py:1024
  (111 other events, 630.3 us)
Sparse Core Ops, SparseCore 0:
  117.0 58.1 all-gather.1
